TPU v7x, 32 devices: a whole 2x2x4 slice. The times are simulated.
32 devices in a mesh: row: 16 (over z, x, core), col: 2 (over y).
Axes of the slice: x: 2, y: 2, z: 4, core: 2. Of those that a mesh axis runs over, the one named last changes fastest.
Arguments:
- vectors: bfloat16 [8, 32768], P(None, ('row', 'col')), may hold values from -6 to 6
- energies: float32 [32768], P(('row', 'col')), may hold values from 0.5 to 6
- tiles: bfloat16 [32768, 4096], P(('row', 'col')), may hold values from -0.25 to 0.25
- tile_rows: int32 [32768], P(('row', 'col')), may hold values from 0 to 31, as said below
- tile_cols: int32 [32768], P(('row', 'col')), may hold values from 0 to 255
- tile_count: int32 [32], P(('row', 'col')), may hold values from 128 to 1024, as said below
Outputs:
- product: bfloat16 [8, 32768], P(None, ('row', 'col'))
- residual: float32 [8, 32768], P(None, ('row', 'col'))
Inputs may be any that keep to these rules, and one draw needn't show every extreme that they name: `tile_count`: every count is at least 128, and some device uses all 1024 slots in every draw; a few devices are full while most use far fewer. `tile_rows`: slots may name the same row and column block more than once; such tiles add.
All inputs are finite; a program needn't handle non-finite values.
Results may differ from a plain program's by a relative error of at most 0.008.
Values may be sent and summed in bfloat16 or wider, within the bound.
No kernel may reach another device: no remote copies, remote signals or barrier semaphores. Data moves between devices by JAX's collectives and lax.ppermute only.
A program may use at most 64 MiB of HBM per device.

v0:
```python
import jax
import jax.numpy as jnp
from jax import lax
from jax.sharding import PartitionSpec as P


def per_device(vectors, energies, tiles, tile_rows, tile_cols, tile_count):
    kvec = vectors.shape[0]
    own_states = vectors.shape[1]
    blk_own = own_states // 64
    n_row = lax.axis_size("row")
    n_col = lax.axis_size("col")
    seg_blocks = n_col * blk_own
    slots = tiles.shape[0]
    group = min(128, slots)
    gathered = lax.all_gather(vectors, "row", axis=1, tiled=True)
    blocks = gathered.reshape(kvec, n_row * blk_own, 64)
    seg_ids = jnp.arange(seg_blocks, dtype=jnp.int32)
    group_ids = jnp.arange(group, dtype=jnp.int32)
    count = tile_count[0]
    turns = (count + group - 1) // group

    def add_group(step, accum):
        first = step * group
        tile_part = lax.dynamic_slice_in_dim(tiles, first, group, 0).reshape(group, 64, 64)
        row_part = lax.dynamic_slice_in_dim(tile_rows, first, group, 0)
        col_part = lax.dynamic_slice_in_dim(tile_cols, first, group, 0)
        picked = jnp.take(blocks, col_part, axis=1)
        prod = jnp.einsum("tji,kti->ktj", tile_part, picked, preferred_element_type=jnp.float32)
        live = first + group_ids < count
        onehot = ((row_part[:, None] == seg_ids[None, :]) & live[:, None]).astype(jnp.bfloat16)
        upper = prod.astype(jnp.bfloat16)
        lower = (prod - upper.astype(jnp.float32)).astype(jnp.bfloat16)
        added = jnp.einsum("ktj,tr->krj", upper, onehot, preferred_element_type=jnp.float32)
        added = added + jnp.einsum("ktj,tr->krj", lower, onehot, preferred_element_type=jnp.float32)
        return accum + added

    accum = jnp.zeros((kvec, seg_blocks, 64), jnp.float32)
    accum = lax.fori_loop(0, turns, add_group, accum)
    partial_value = accum.reshape(kvec, seg_blocks * 64)
    summed = lax.psum(partial_value.astype(jnp.bfloat16), "col").astype(jnp.float32)
    share = lax.dynamic_slice_in_dim(summed, lax.axis_index("col") * own_states, own_states, 1)
    vec32 = vectors.astype(jnp.float32)
    diag_part = energies[None, :] * vec32
    whole = diag_part + share
    terms = jnp.einsum("an,bn->ab", vec32, whole, precision=lax.Precision.HIGHEST)
    total_states = n_row * n_col * own_states
    gram = lax.psum(terms, ("row", "col")) / total_states
    residual = whole - jnp.einsum("ab,an->bn", gram, vec32, precision=lax.Precision.HIGHEST)
    return (whole.astype(jnp.bfloat16), residual)


def solution(mesh):
    in_specs = (
        P(None, ("row", "col")),
        P(("row", "col")),
        P(("row", "col"), None),
        P(("row", "col")),
        P(("row", "col")),
        P(("row", "col")),
    )
    out_specs = (P(None, ("row", "col")), P(None, ("row", "col")))
    return jax.shard_map(
        per_device, mesh=mesh, in_specs=in_specs, out_specs=out_specs, check_vma=False
    )
```

profile of v0, /device:TPU:0, one launch (start us, length us, event | category | flops | bytes accessed | tf_op | source)
XLA Modules:
  0.0 159.3 jit_solution(9749205594047981277)
XLA Ops:
  1.3 24.0 %all_gather.3 = bf16[8,16384]{1,0:T(8,128)(2,1)S(1)} all-gather(bf16[8,1024]{1,0:T(8,128)(2,1)} %param.8), channel_id=1, replica_groups=mesh['row'=16,'col'=2] {'row'}, dimensions={1}, use_global_device_ids=true | all-gather | bytes 278528 | tf_op jit(solution)/shard_map/all_gather | solution.py:16
  27.0 86.8 %while.11 = (s32[]{:T(128)}, f32[8,32,64]{2,1,0:T(8,128)S(1)}, s32[]{:T(128)}, s32[1024]{0:T(1024)}, s32[]{:T(128)}, /*index=5*/s32[1024]{0:T(1024)}, bf16[8,256...) while((s32[]{:T(128)}, f32[8,32,64]{2,1,0:T(8,128)S(1)}, ...), condition=%wide.region_1.2_spmd.clone, body=%wide.region_0.1_spmd.clone.sunk | while | flops 17156100 | bytes 9315135 | solution.py:39
  27.8 1.4 compare_and_fusion.2
  29.2 1.3 constant_dynamic-slice_fusion.2
  31.2 3.0 %copy.25 = bf16[128,64,64]{2,1,0:T(8,128)(2,1)S(1)} copy(bf16[128,64,64]{0,2,1:T(8,128)(2,1)S(1)} %bitcast.56) | data formatting | bytes 2097152 | tf_op jit(solution)/shard_map/while/body/reshape | solution.py:25
  34.2 1.7 %gather_fusion = bf16[128,8,64]{2,1,0:T(8,128)(2,1)S(1)} fusion(bf16[8,256,64]{2,0,1:T(8,128)(2,1)} %get-tuple-element.197, s32[1024]{0:T(1024)S(1)} %pad_clamp_fusion.2), kind=kCustom, calls=%fused_computation.clone.clone.1 | custom fusion | bytes 262656 | tf_op jit(solution)/shard_map/while/body/jit(_take)/gather | solution.py:28
  38.7 1.4 compare_and_fusion.2
  40.1 1.3 constant_dynamic-slice_fusion.2
  42.0 3.0 %copy.25 = bf16[128,64,64]{2,1,0:T(8,128)(2,1)S(1)} copy(bf16[128,64,64]{0,2,1:T(8,128)(2,1)S(1)} %bitcast.56) | data formatting | bytes 2097152 | tf_op jit(solution)/shard_map/while/body/reshape | solution.py:25
  45.1 1.7 %gather_fusion = bf16[128,8,64]{2,1,0:T(8,128)(2,1)S(1)} fusion(bf16[8,256,64]{2,0,1:T(8,128)(2,1)} %get-tuple-element.197, s32[1024]{0:T(1024)S(1)} %pad_clamp_fusion.2), kind=kCustom, calls=%fused_computation.clone.clone.1 | custom fusion | bytes 262656 | tf_op jit(solution)/shard_map/while/body/jit(_take)/gather | solution.py:28
  49.5 1.4 compare_and_fusion.2
  50.9 1.3 constant_dynamic-slice_fusion.2
  52.9 3.0 %copy.25 = bf16[128,64,64]{2,1,0:T(8,128)(2,1)S(1)} copy(bf16[128,64,64]{0,2,1:T(8,128)(2,1)S(1)} %bitcast.56) | data formatting | bytes 2097152 | tf_op jit(solution)/shard_map/while/body/reshape | solution.py:25
  55.9 1.7 %gather_fusion = bf16[128,8,64]{2,1,0:T(8,128)(2,1)S(1)} fusion(bf16[8,256,64]{2,0,1:T(8,128)(2,1)} %get-tuple-element.197, s32[1024]{0:T(1024)S(1)} %pad_clamp_fusion.2), kind=kCustom, calls=%fused_computation.clone.clone.1 | custom fusion | bytes 262656 | tf_op jit(solution)/shard_map/while/body/jit(_take)/gather | solution.py:28
  60.4 1.4 compare_and_fusion.2
  61.8 1.3 constant_dynamic-slice_fusion.2
  63.7 3.0 %copy.25 = bf16[128,64,64]{2,1,0:T(8,128)(2,1)S(1)} copy(bf16[128,64,64]{0,2,1:T(8,128)(2,1)S(1)} %bitcast.56) | data formatting | bytes 2097152 | tf_op jit(solution)/shard_map/while/body/reshape | solution.py:25
  66.7 1.7 %gather_fusion = bf16[128,8,64]{2,1,0:T(8,128)(2,1)S(1)} fusion(bf16[8,256,64]{2,0,1:T(8,128)(2,1)} %get-tuple-element.197, s32[1024]{0:T(1024)S(1)} %pad_clamp_fusion.2), kind=kCustom, calls=%fused_computation.clone.clone.1 | custom fusion | bytes 262656 | tf_op jit(solution)/shard_map/while/body/jit(_take)/gather | solution.py:28
  71.2 1.4 compare_and_fusion.2
  74.6 3.0 %copy.25 = bf16[128,64,64]{2,1,0:T(8,128)(2,1)S(1)} copy(bf16[128,64,64]{0,2,1:T(8,128)(2,1)S(1)} %bitcast.56) | data formatting | bytes 2097152 | tf_op jit(solution)/shard_map/while/body/reshape | solution.py:25
  77.6 1.7 %gather_fusion = bf16[128,8,64]{2,1,0:T(8,128)(2,1)S(1)} fusion(bf16[8,256,64]{2,0,1:T(8,128)(2,1)} %get-tuple-element.197, s32[1024]{0:T(1024)S(1)} %pad_clamp_fusion.2), kind=kCustom, calls=%fused_computation.clone.clone.1 | custom fusion | bytes 262656 | tf_op jit(solution)/shard_map/while/body/jit(_take)/gather | solution.py:28
  82.0 1.4 compare_and_fusion.2
  85.4 3.0 %copy.25 = bf16[128,64,64]{2,1,0:T(8,128)(2,1)S(1)} copy(bf16[128,64,64]{0,2,1:T(8,128)(2,1)S(1)} %bitcast.56) | data formatting | bytes 2097152 | tf_op jit(solution)/shard_map/while/body/reshape | solution.py:25
  88.4 1.7 %gather_fusion = bf16[128,8,64]{2,1,0:T(8,128)(2,1)S(1)} fusion(bf16[8,256,64]{2,0,1:T(8,128)(2,1)} %get-tuple-element.197, s32[1024]{0:T(1024)S(1)} %pad_clamp_fusion.2), kind=kCustom, calls=%fused_computation.clone.clone.1 | custom fusion | bytes 262656 | tf_op jit(solution)/shard_map/while/body/jit(_take)/gather | solution.py:28
  92.9 1.4 compare_and_fusion.2
  96.3 3.0 %copy.25 = bf16[128,64,64]{2,1,0:T(8,128)(2,1)S(1)} copy(bf16[128,64,64]{0,2,1:T(8,128)(2,1)S(1)} %bitcast.56) | data formatting | bytes 2097152 | tf_op jit(solution)/shard_map/while/body/reshape | solution.py:25
  99.3 1.7 %gather_fusion = bf16[128,8,64]{2,1,0:T(8,128)(2,1)S(1)} fusion(bf16[8,256,64]{2,0,1:T(8,128)(2,1)} %get-tuple-element.197, s32[1024]{0:T(1024)S(1)} %pad_clamp_fusion.2), kind=kCustom, calls=%fused_computation.clone.clone.1 | custom fusion | bytes 262656 | tf_op jit(solution)/shard_map/while/body/jit(_take)/gather | solution.py:28
  103.7 1.4 compare_and_fusion.2
  107.1 3.0 %copy.25 = bf16[128,64,64]{2,1,0:T(8,128)(2,1)S(1)} copy(bf16[128,64,64]{0,2,1:T(8,128)(2,1)S(1)} %bitcast.56) | data formatting | bytes 2097152 | tf_op jit(solution)/shard_map/while/body/reshape | solution.py:25
  110.1 1.7 %gather_fusion = bf16[128,8,64]{2,1,0:T(8,128)(2,1)S(1)} fusion(bf16[8,256,64]{2,0,1:T(8,128)(2,1)} %get-tuple-element.197, s32[1024]{0:T(1024)S(1)} %pad_clamp_fusion.2), kind=kCustom, calls=%fused_computation.clone.clone.1 | custom fusion | bytes 262656 | tf_op jit(solution)/shard_map/while/body/jit(_take)/gather | solution.py:28
  113.9 6.9 %psum.14 = bf16[8,2048]{1,0:T(8,128)(2,1)S(1)} all-reduce(bf16[8,2048]{1,0:T(8,128)(2,1)S(1)} %convert_element_type.27), channel_id=1, replica_groups=mesh['row'=16,'col'=2] {'col'}, use_global_device_ids=true, to_apply=%region_2.3 | all-reduce | flops 16384 | bytes 65536 | tf_op jit(solution)/shard_map/psum | solution.py:41
  121.6 36.9 %psum.15 = f32[8,8]{0,1:T(8,128)S(1)} all-reduce(f32[8,8]{0,1:T(8,128)S(1)} %convolution_bitcast_fusion), channel_id=1, replica_groups=mesh['row'=16,'col'=2] {'row','col'}, use_global_device_ids=true, to_apply=%region_3.4 | all-reduce | flops 64 | bytes 512 | tf_op jit(solution)/shard_map/psum | solution.py:48
  (72 shorter events, 35.5 us)
Async XLA Ops:
  27.0 93.9 %copy-start = (bf16[8,1024]{1,0:T(8,128)(2,1)S(1)}, bf16[8,1024]{1,0:T(8,128)(2,1)}, u32[]{:S(2)}) copy-start(bf16[8,1024]{1,0:T(8,128)(2,1)} %param.8) | copy-start | bytes 49156
  27.0 93.9 %copy-start.1 = (f32[1024]{0:T(1024)S(1)}, f32[1024]{0:T(1024)}, u32[]{:S(2)}) copy-start(f32[1024]{0:T(1024)} %param.9) | copy-start | bytes 12292
where the time goes:
time: 162 us; the launch traced here: 159 us
  blocking collectives  67.9 us (42%)
  local copies, waits for them, and re-layouts  63 us (39%)
  matrix products  14.6 us (9%)
  other arithmetic  12 us (7%)
    psum x1, blocking collectives, per_device(): gram = lax.psum(terms, ('row', 'col')) / total_states  36.9 us
    all_gather x1, blocking collectives, per_device(): gathered = lax.all_gather(vectors, 'row', axis=1, tiled=True)  24 us
    reshape x8, local copies, waits for them, and re-layouts, add_group(): lax.dynamic_slice_in_dim(tiles, first, group, 0).reshape(group, 64, 64)  23.9 us
    dynamic_slice x16, local copies, waits for them, and re-layouts, add_group(): lax.dynamic_slice_in_dim(tiles, first, group, 0).reshape(group, 64, 64)  15.6 us
    gather x8, local copies, waits for them, and re-layouts, add_group(): picked = jnp.take(blocks, col_part, axis=1)  13.7 us
    and x8, other arithmetic, add_group(): picked = jnp.take(blocks, col_part, axis=1)  11.3 us
    dot_general x8, matrix products, add_group(): jnp.einsum('tji,kti->ktj', tile_part, picked, preferred_element_type=jnp....  9.87 us
    psum x1, blocking collectives, per_device(): lax.psum(partial_value.astype(jnp.bfloat16), 'col').astype(jnp.float32)  6.91 us

commit v1 on v0

v1 whole, which is shorter than its diff:
```python
import functools
import math

import jax
import jax.numpy as jnp
from jax import lax
from jax.experimental import pallas as pl
from jax.experimental.pallas import tpu as pltpu
from jax.sharding import PartitionSpec as P

LANES = 128
SUB = 8
CHUNK = 64

NT = (((1,), (1,)), ((), ()))


def tile_kernel(
    n_col, side, rows_s, cols_s, info_s, gath, seg, ener, tiles,
    own_ref, send_ref, terms_ref, buf, table, picked, part, sems, *acc,
):
    n_row, kvec, own = gath.shape
    slots = tiles.shape[0]
    blk_own = own // side
    per = LANES // side
    chunks = slots // CHUNK
    n_chunk = tiles.shape[1] // LANES
    count = info_s[0]
    my_col = info_s[1]

    def tile_copy(ch):
        span = pl.ds(pl.multiple_of(ch * CHUNK, CHUNK), CHUNK)
        return pltpu.make_async_copy(tiles.at[span], buf.at[span], sems.at[ch])

    used = (count + CHUNK - 1) // CHUNK

    def start(ch, carry):
        tile_copy(ch).start()
        return carry

    lax.fori_loop(0, used, start, 0)

    lane = lax.broadcasted_iota(jnp.int32, (kvec, LANES), 1)
    low = lane < side
    zero = jnp.zeros((kvec, LANES), jnp.float32)

    def fill(r, carry):
        for p in range(own // LANES):
            x = gath[r, :, p * LANES:(p + 1) * LANES].astype(jnp.float32)
            y = pltpu.roll(x, side, 1)
            at = r * blk_own + p * per
            even = jnp.concatenate([jnp.where(low, x, zero), jnp.where(low, zero, y)], axis=0)
            odd = jnp.concatenate([jnp.where(low, y, zero), jnp.where(low, zero, x)], axis=0)
            table[at] = even.astype(jnp.bfloat16)
            table[at + 1] = odd.astype(jnp.bfloat16)
        return carry

    lax.fori_loop(0, n_row, fill, 0)
    table[n_row * blk_own] = jnp.zeros((per * kvec, LANES), jnp.bfloat16)

    n_seg = acc[0].shape[0]

    def clear(r, carry):
        for a in acc:
            a[r] = jnp.zeros(a.shape[1:], jnp.float32)
        return carry

    lax.fori_loop(0, n_seg, clear, 0)

    rows_of = per * kvec

    def one_chunk(ch, carry):
        tile_copy(ch).wait()

        def pair(q, inner):
            base = pl.multiple_of(ch * CHUNK + q * 2 * SUB, 2 * SUB)
            x = buf[pl.ds(base, 2 * SUB), :].astype(jnp.float32)
            for h in range(2):
                xh = x[h * SUB:(h + 1) * SUB]
                w = jnp.concatenate(
                    [xh[:, c * LANES:(c + 1) * LANES] for c in range(n_chunk)], axis=0
                ).astype(jnp.bfloat16)
                left = jnp.concatenate(
                    [table[cols_s[base + h * SUB + t]] for t in range(SUB)], axis=0
                )
                out = lax.dot_general(left, w, NT, preferred_element_type=jnp.float32)
                for t in range(SUB):
                    r = rows_s[base + h * SUB + t]
                    acc[t][r] += out[t * rows_of:(t + 1) * rows_of]
            return inner

        lax.fori_loop(0, CHUNK // (2 * SUB), pair, 0)
        return carry

    lax.fori_loop(0, used, one_chunk, 0)

    width = n_chunk * SUB
    lane_w = lax.broadcasted_iota(jnp.int32, (rows_of, width), 1)

    def pick(m, carry):
        pieces = []
        for par in range(per):
            total = jnp.zeros((rows_of, width), jnp.float32)
            for t in range(SUB):
                total = jnp.where(lane_w % SUB == t, acc[t][m * per + par], total)
            for jp in range(per):
                pieces.append(total[jp * kvec:(jp + 1) * kvec])
        a = jnp.concatenate(pieces, axis=1)
        hi = a.astype(jnp.bfloat16).astype(jnp.float32)
        both = jnp.concatenate([hi, a - hi], axis=0).astype(jnp.bfloat16)
        picked[pl.ds(pl.multiple_of(m * 2 * kvec, 2 * kvec), 2 * kvec), :] = both
        return carry

    pairs = n_seg // per
    lax.fori_loop(0, pairs, pick, 0)

    depth = per * per * width
    k_id = lax.broadcasted_iota(jnp.int32, (depth, LANES), 0)
    n_id = lax.broadcasted_iota(jnp.int32, (depth, LANES), 1)
    par_id = k_id // (per * width)
    jp_id = (k_id // width) % per
    c_id = (k_id % width) // SUB
    select = (n_id == side * par_id + per * c_id + jp_id).astype(jnp.float32).astype(jnp.bfloat16)
    spread = jnp.dot(picked[...], select, preferred_element_type=jnp.float32)
    for m in range(pairs):
        at = m * 2 * kvec
        row = spread[at:at + kvec] + spread[at + kvec:at + 2 * kvec]
        c, lane0 = divmod(m * LANES, own)
        part[c, :, lane0:lane0 + LANES] = row

    mine = seg[my_col].astype(jnp.float32)
    base = part[my_col] + ener[...] * mine
    part[my_col] = base
    own_ref[...] = base
    for s in range(1, n_col):
        send_ref[s - 1] = part[(my_col + s) % n_col].astype(jnp.bfloat16)
    terms = jnp.zeros((kvec, kvec), jnp.float32)
    for c in range(n_col):
        terms = terms + lax.dot_general(
            seg[c].astype(jnp.float32), part[c], NT,
            precision=lax.Precision.HIGHEST, preferred_element_type=jnp.float32,
        )
    terms_ref[...] = terms


def tile_work(n_col, rows, cols, info, gath, seg, ener, tiles):
    n_row, kvec, own = gath.shape
    slots, area = tiles.shape
    side = math.isqrt(area)
    per = LANES // side
    blk_own = own // side
    n_seg = n_col * blk_own
    width = area // LANES * SUB
    vmem = pl.BlockSpec(memory_space=pltpu.VMEM)
    smem = pl.BlockSpec(memory_space=pltpu.SMEM)
    return pl.pallas_call(
        functools.partial(tile_kernel, n_col, side),
        out_shape=(
            jax.ShapeDtypeStruct((kvec, own), jnp.float32),
            jax.ShapeDtypeStruct((n_col - 1, kvec, own), jnp.bfloat16),
            jax.ShapeDtypeStruct((kvec, kvec), jnp.float32),
        ),
        in_specs=[smem, smem, smem, vmem, vmem, vmem, pl.BlockSpec(memory_space=pl.ANY)],
        out_specs=(vmem, vmem, vmem),
        scratch_shapes=[
            pltpu.VMEM((slots, area), jnp.bfloat16),
            pltpu.VMEM((n_row * blk_own + 1, per * kvec, LANES), jnp.bfloat16),
            pltpu.VMEM((n_seg // per * 2 * kvec, per * per * width), jnp.bfloat16),
            pltpu.VMEM((n_col, kvec, own), jnp.float32),
            pltpu.SemaphoreType.DMA((slots // CHUNK,)),
        ] + [pltpu.VMEM((n_seg, per * kvec, width), jnp.float32)] * SUB,
        compiler_params=pltpu.CompilerParams(vmem_limit_bytes=48 * 2**20),
        cost_estimate=pl.CostEstimate(
            flops=2 * slots * area * kvec, bytes_accessed=2 * slots * area, transcendentals=0
        ),
        name="tile_work",
    )(rows, cols, info, gath, seg, ener, tiles)


def sum_everywhere(x, axes, size):
    if size & (size - 1):
        return lax.psum(x, axes)
    step = 1
    while step < size:
        x = x + lax.ppermute(x, axes, [(i, i ^ step) for i in range(size)])
        step *= 2
    return x


def per_device(vectors, energies, tiles, tile_rows, tile_cols, tile_count):
    kvec, own = vectors.shape
    n_row = lax.axis_size("row")
    n_col = lax.axis_size("col")
    slots, area = tiles.shape
    side = math.isqrt(area)
    n_blocks = n_row * (own // side)
    gath = lax.all_gather(vectors, "row", axis=0)
    seg = lax.all_gather(vectors, "col", axis=0)
    live = jnp.arange(slots, dtype=jnp.int32) < tile_count[0]
    cols = jnp.where(live, tile_cols, n_blocks)
    info = jnp.stack([tile_count[0], lax.axis_index("col").astype(jnp.int32)])
    base, send, terms = tile_work(n_col, tile_rows, cols, info, gath, seg, energies[None, :], tiles)
    gram = sum_everywhere(terms, ("row", "col"), n_row * n_col) / (n_row * n_col * own)
    whole = base
    for s in range(1, n_col):
        got = lax.ppermute(send[s - 1], "col", [(c, (c + s) % n_col) for c in range(n_col)])
        whole = whole + got.astype(jnp.float32)
    vec32 = vectors.astype(jnp.float32)
    residual = whole - jnp.einsum("ab,an->bn", gram, vec32, precision=lax.Precision.HIGHEST)
    return (whole.astype(jnp.bfloat16), residual)


def solution(mesh):
    in_specs = (
        P(None, ("row", "col")),
        P(("row", "col")),
        P(("row", "col"), None),
        P(("row", "col")),
        P(("row", "col")),
        P(("row", "col")),
    )
    out_specs = (P(None, ("row", "col")), P(None, ("row", "col")))
    return jax.shard_map(
        per_device, mesh=mesh, in_specs=in_specs, out_specs=out_specs, check_vma=False
    )
```

time: 162 us -> 61.9 us (0.38); the launches traced: 159 us -> 61.6 us
  local copies, waits for them, and re-layouts: 63 us -> 1.38 us
  blocking collectives: 67.9 us -> 28.6 us
  matrix products: 14.6 us -> 0.82 us
  waiting for transfers between devices: 0 us -> 11.3 us
  other arithmetic: 12 us -> 1.39 us
  Pallas kernels: 0 us -> 9.04 us
  starting transfers between devices: 0 us -> 7.75 us
    psum x2 -> x0, blocking collectives: 43.8 us -> none  [the longest x1 36.9 us: per_device(): gram = lax.psum(terms, ('row', 'col')) / total_states]
    reshape x9 -> x0, local copies, waits for them, and re-layouts: 24.4 us -> none  [the longest x8 23.9 us: add_group(): lax.dynamic_slice_in_dim(tiles, first, group, 0).reshape(group, 64, 64)]
    dynamic_slice x24 -> x0, local copies, waits for them, and re-layouts: 21.8 us -> none  [the longest x16 15.6 us: add_group(): lax.dynamic_slice_in_dim(tiles, first, group, 0).reshape(group, 64, 64)]
    dot_general x25 -> x0, matrix products: 13.9 us -> none  [the longest x8 9.87 us: add_group(): jnp.einsum('tji,kti->ktj', tile_part, picked, preferred_element_type=jnp....]
    gather x8 -> x0, local copies, waits for them, and re-layouts: 13.7 us -> none  [add_group(): picked = jnp.take(blocks, col_part, axis=1)]
    and x8 -> x0, other arithmetic: 11.3 us -> none  [add_group(): picked = jnp.take(blocks, col_part, axis=1)]
    ppermute x0 -> x6, waiting for transfers between devices: none -> 11.3 us  [the longest x5 11.3 us: sum_everywhere(): x = x + lax.ppermute(x, axes, [(i, i ^ step) for i in range(size)])]
    pallas_call x0 -> x1, Pallas kernels: none -> 9.04 us  [tile_work(): pl.pallas_call(functools.partial(tile_kernel, n_col, side), out_shape=(ja...]
  transfers between devices with their start and end apart: 0 -> 6, of which waited for: 0 -> 5; matrix products, arithmetic and copies ran while one was open for 0% -> 1% of each run, Pallas kernels for 0% -> 0%
where the time goes in v1:
time: 61.9 us; the launch traced here: 61.6 us
  blocking collectives  28.6 us (46%)
  waiting for transfers between devices  11.3 us (18%)
  Pallas kernels  9.04 us (15%)
  starting transfers between devices  7.75 us (13%)
  other arithmetic  1.39 us (2%)
  local copies, waits for them, and re-layouts  1.38 us (2%)
  between operations  1.31 us (2%)
  matrix products  0.82 us (1%)
    all_gather x1, blocking collectives, per_device(): gath = lax.all_gather(vectors, 'row', axis=0)  23 us
    ppermute x5, waiting for transfers between devices, sum_everywhere(): x = x + lax.ppermute(x, axes, [(i, i ^ step) for i in range(size)])  11.3 us
    pallas_call x1, Pallas kernels, tile_work(): pl.pallas_call(functools.partial(tile_kernel, n_col, side), out_shape=(ja...  9.04 us
    ppermute x5, starting transfers between devices, sum_everywhere(): x = x + lax.ppermute(x, axes, [(i, i ^ step) for i in range(size)])  6.96 us
    all_gather x1, blocking collectives, per_device(): seg = lax.all_gather(vectors, 'col', axis=0)  5.61 us
    unnamed x6, local copies, waits for them, and re-layouts  1.38 us
  transfers between devices with their start and end apart: 6, of which 5 were waited for; matrix products, arithmetic and copies ran while one was open for 1% of the time, Pallas kernels for 0%

profile of v1, /device:TPU:0, one launch (start us, length us, event | category | flops | bytes accessed | tf_op | source)
XLA Modules:
  0.0 61.6 jit_solution(10702087774346404198)
XLA Ops:
  0.6 0.0 copy-start.2
  0.6 5.6 %all-gather.1 = bf16[16,1024]{1,0:T(8,128)(2,1)S(1)} all-gather(bf16[8,1024]{1,0:T(8,128)(2,1)} %param.6), channel_id=3, replica_groups=mesh['row'=16,'col'=2] {'col'}, dimensions={0}, use_global_device_ids=true | all-gather | bytes 49152 | tf_op jit(solution)/shard_map/all_gather | solution.py:198
  6.3 23.0 %all-gather = bf16[128,1024]{1,0:T(8,128)(2,1)S(1)} all-gather(bf16[8,1024]{1,0:T(8,128)(2,1)} %param.6), channel_id=2, replica_groups=mesh['row'=16,'col'=2] {'row'}, dimensions={0}, use_global_device_ids=true | all-gather | bytes 278528 | tf_op jit(solution)/shard_map/all_gather | solution.py:197
  29.9 0.1 pad_add_fusion.info_s
  30.0 0.7 %fusion.3.cols_s = s32[1024]{0:T(1024)S(1)} fusion(s32[1024]{0:T(1024)} %param.10, s32[]{:T(128)} %bitcast.7), kind=kLoop, calls=%fused_computation.6 | loop fusion | flops 2048 | bytes 8196 | tf_op jit(solution)/shard_map/jit(_where)/select_n | solution.py:200
  30.7 0.0 copy-start
  30.7 0.7 %copy-done = s32[1024]{0:T(1024)S(1)} copy-done((s32[1024]{0:T(1024)S(1)}, s32[1024]{0:T(1024)}, u32[]{:S(2)}) %copy-start) | copy-done | bytes 4120
  31.4 0.0 copy-start.1
  31.4 0.7 %copy-done.1 = f32[1024]{0:T(1024)S(1)} copy-done((f32[1024]{0:T(1024)S(1)}, f32[1024]{0:T(1024)}, u32[]{:S(2)}) %copy-start.1) | copy-done | bytes 4120
  32.1 9.0 %tile_work.1 = (f32[8,1024]{1,0:T(8,128)S(1)}, bf16[1,8,1024]{2,1,0:T(8,128)(2,1)S(1)}, f32[8,8]{1,0:T(8,128)S(1)}) custom-call(s32[1024]{0:T(1024)S(1)} %copy-done, s32[1024]{0:T(1024)S(1)} %fusion.3.cols_s, s32[2]{0:T(128)S(1)} %pad_add_fusion.info_s, bf16[16,8,1024]{2,1,0:T(8,128)(2,1)S(1)} %bitcast.8, bf16[2,8,1024]{2,1,0:T(8,128)(2,1)S(1)} %bitcast.9, ...), custom_call_target="tpu_custom_call" | custom-call | flops 67108864 | bytes 8388608 | tf_op jit(solution)/shard_map/tile_work/pallas_call | solution.py:156
  41.1 0.8 %collective-permute-start = (bf16[8,1024]{1,0:T(8,128)(2,1)S(1)}, bf16[8,1024]{1,0:T(8,128)(2,1)S(1)}, u32[]{:S(2)}, u32[]{:S(2)}) collective-permute-start(bf16[8,1024]{1,0:T(8,128)(2,1)S(1)} %bitcast.11), channel_id=1, source_target_pairs={{0,1},{1,0},{2,3},{3,2},{4,5},{5,4},{6,7},{7,6},{8,9},{9,8},{10,11... | collective-permute-start | bytes 49160 | tf_op jit(solution)/shard_map/ppermute | solution.py:206
  41.9 1.3 %collective-permute-start.1 = (f32[8,8]{1,0:T(8,128)S(1)}, f32[8,8]{1,0:T(8,128)S(1)}, u32[]{:S(2)}, u32[]{:S(2)}) collective-permute-start(f32[8,8]{1,0:T(8,128)S(1)} %get-tuple-element.7), channel_id=1, source_target_pairs={{0,1},{1,0},{2,3},{3,2},{4,5},{5,4},{6,7},{7,6},{8,9},{9,8},{10,11... | collective-permute-start | bytes 776 | tf_op jit(solution)/shard_map/ppermute | solution.py:185
  43.2 2.3 %collective-permute-done.1 = f32[8,8]{1,0:T(8,128)S(1)} collective-permute-done((f32[8,8]{1,0:T(8,128)S(1)}, f32[8,8]{1,0:T(8,128)S(1)}, u32[]{:S(2)}, u32[]{:S(2)}) %collective-permute-start.1) | collective-permute-done | bytes 288 | tf_op jit(solution)/shard_map/ppermute | solution.py:185
  45.5 0.0 collective-permute-start.2
  45.5 1.2 %collective-permute-done.2 = f32[8,8]{1,0:T(8,128)S(1)} collective-permute-done((f32[8,8]{1,0:T(8,128)S(1)}, f32[8,8]{1,0:T(8,128)S(1)}, u32[]{:S(2)}, u32[]{:S(2)}) %collective-permute-start.2) | collective-permute-done | bytes 288 | tf_op jit(solution)/shard_map/ppermute | solution.py:185
  46.7 0.0 collective-permute-start.3
  46.7 3.6 %collective-permute-done.3 = f32[8,8]{1,0:T(8,128)S(1)} collective-permute-done((f32[8,8]{1,0:T(8,128)S(1)}, f32[8,8]{1,0:T(8,128)S(1)}, u32[]{:S(2)}, u32[]{:S(2)}) %collective-permute-start.3) | collective-permute-done | bytes 288 | tf_op jit(solution)/shard_map/ppermute | solution.py:185
  50.3 0.4 collective-permute-start.4
  50.7 3.2 %collective-permute-done.4 = f32[8,8]{1,0:T(8,128)S(1)} collective-permute-done((f32[8,8]{1,0:T(8,128)S(1)}, f32[8,8]{1,0:T(8,128)S(1)}, u32[]{:S(2)}, u32[]{:S(2)}) %collective-permute-start.4) | collective-permute-done | bytes 288 | tf_op jit(solution)/shard_map/ppermute | solution.py:185
  53.9 5.3 %collective-permute-start.5 = (f32[8,8]{1,0:T(8,128)S(1)}, f32[8,8]{1,0:T(8,128)S(1)}, u32[]{:S(2)}, u32[]{:S(2)}) collective-permute-start(f32[8,8]{1,0:T(8,128)S(1)} %add.22), channel_id=1, source_target_pairs={{0,16},{1,17},{2,18},{3,19},{4,20},{5,21},{6,22},{7,23},{8,24},{9,... | collective-permute-start | bytes 776 | tf_op jit(solution)/shard_map/ppermute | solution.py:185
  59.2 0.0 collective-permute-done
  59.2 0.6 fusion
  59.8 1.0 %collective-permute-done.5 = f32[8,8]{1,0:T(8,128)S(1)} collective-permute-done((f32[8,8]{1,0:T(8,128)S(1)}, f32[8,8]{1,0:T(8,128)S(1)}, u32[]{:S(2)}, u32[]{:S(2)}) %collective-permute-start.5) | collective-permute-done | bytes 288 | tf_op jit(solution)/shard_map/ppermute | solution.py:185
  60.8 0.0 copy-done.2
  60.8 0.8 %convolution_subtract_fusion = f32[8,1024]{1,0:T(8,128)} fusion(bf16[8,1024]{1,0:T(8,128)(2,1)S(1)} %copy-done.2, f32[8,1024]{1,0:T(8,128)S(1)} %get-tuple-element.5, bf16[8,1024]{1,0:T(8,128)(2,1)S(1)} %collective-permute-done, f32[8,8]{1,0:T(8,128)S(1)} %add.22, f32[8,8]{1,0:T(8,128)S(1)} %collective-permute-done.5), kind=kOutput, calls=%fused_computation | convolution fusion | flops 811136 | bytes 98816 | tf_op jit(solution)/shard_map/ab,an->bn/dot_general | solution.py:209
  (4 shorter events, 0.0 us)
Async XLA Ops:
  0.6 60.2 %copy-start.2 = (bf16[8,1024]{1,0:T(8,128)(2,1)S(1)}, bf16[8,1024]{1,0:T(8,128)(2,1)}, u32[]{:S(2)}) copy-start(bf16[8,1024]{1,0:T(8,128)(2,1)} %param.6) | copy-start | bytes 49156
  30.7 0.7 %copy-start = (s32[1024]{0:T(1024)S(1)}, s32[1024]{0:T(1024)}, u32[]{:S(2)}) copy-start(s32[1024]{0:T(1024)} %rows_s.1) | copy-start | bytes 12292
  31.4 0.7 %copy-start.1 = (f32[1024]{0:T(1024)S(1)}, f32[1024]{0:T(1024)}, u32[]{:S(2)}) copy-start(f32[1024]{0:T(1024)} %param.7) | copy-start | bytes 12292
  41.1 18.1 %collective-permute-start = (bf16[8,1024]{1,0:T(8,128)(2,1)S(1)}, bf16[8,1024]{1,0:T(8,128)(2,1)S(1)}, u32[]{:S(2)}, u32[]{:S(2)}) collective-permute-start(bf16[8,1024]{1,0:T(8,128)(2,1)S(1)} %bitcast.11), channel_id=1, source_target_pairs={{0,1},{1,0},{2,3},{3,2},{4,5},{5,4},{6,7},{7,6},{8,9},{9,8},{10,11... | collective-permute-start | bytes 49160 | tf_op jit(solution)/shard_map/ppermute | solution.py:206
  41.9 3.6 %collective-permute-start.1 = (f32[8,8]{1,0:T(8,128)S(1)}, f32[8,8]{1,0:T(8,128)S(1)}, u32[]{:S(2)}, u32[]{:S(2)}) collective-permute-start(f32[8,8]{1,0:T(8,128)S(1)} %get-tuple-element.7), channel_id=1, source_target_pairs={{0,1},{1,0},{2,3},{3,2},{4,5},{5,4},{6,7},{7,6},{8,9},{9,8},{10,11... | collective-permute-start | bytes 776 | tf_op jit(solution)/shard_map/ppermute | solution.py:185
  45.5 1.2 %collective-permute-start.2 = (f32[8,8]{1,0:T(8,128)S(1)}, f32[8,8]{1,0:T(8,128)S(1)}, u32[]{:S(2)}, u32[]{:S(2)}) collective-permute-start(f32[8,8]{1,0:T(8,128)S(1)} %add.19), channel_id=1, source_target_pairs={{0,2},{1,3},{2,0},{3,1},{4,6},{5,7},{6,4},{7,5},{8,10},{9,11},{10,... | collective-permute-start | bytes 776 | tf_op jit(solution)/shard_map/ppermute | solution.py:185
  46.7 3.6 %collective-permute-start.3 = (f32[8,8]{1,0:T(8,128)S(1)}, f32[8,8]{1,0:T(8,128)S(1)}, u32[]{:S(2)}, u32[]{:S(2)}) collective-permute-start(f32[8,8]{1,0:T(8,128)S(1)} %add.20), channel_id=1, source_target_pairs={{0,4},{1,5},{2,6},{3,7},{4,0},{5,1},{6,2},{7,3},{8,12},{9,13},{10,... | collective-permute-start | bytes 776 | tf_op jit(solution)/shard_map/ppermute | solution.py:185
  50.3 3.6 %collective-permute-start.4 = (f32[8,8]{1,0:T(8,128)S(1)}, f32[8,8]{1,0:T(8,128)S(1)}, u32[]{:S(2)}, u32[]{:S(2)}) collective-permute-start(f32[8,8]{1,0:T(8,128)S(1)} %add.21), channel_id=1, source_target_pairs={{0,8},{1,9},{2,10},{3,11},{4,12},{5,13},{6,14},{7,15},{8,0},{9,1},... | collective-permute-start | bytes 776 | tf_op jit(solution)/shard_map/ppermute | solution.py:185
  53.9 6.9 %collective-permute-start.5 = (f32[8,8]{1,0:T(8,128)S(1)}, f32[8,8]{1,0:T(8,128)S(1)}, u32[]{:S(2)}, u32[]{:S(2)}) collective-permute-start(f32[8,8]{1,0:T(8,128)S(1)} %add.22), channel_id=1, source_target_pairs={{0,16},{1,17},{2,18},{3,19},{4,20},{5,21},{6,22},{7,23},{8,24},{9,... | collective-permute-start | bytes 776 | tf_op jit(solution)/shard_map/ppermute | solution.py:185

commit v2 on v1

v2 whole, which is shorter than its diff:
```python
import functools
import math

import jax
import jax.numpy as jnp
from jax import lax
from jax.experimental import pallas as pl
from jax.experimental.pallas import tpu as pltpu
from jax.sharding import PartitionSpec as P

LANES = 128
SUB = 8
CHUNK = 64
WIDEST = 32

NT = (((1,), (1,)), ((), ()))


def tile_kernel(
    n_row, n_col, side, rows_s, cols_s, count_s, ener, tiles, *refs,
):
    gath, refs = refs[:n_row], refs[n_row:]
    seg, refs = refs[:n_col], refs[n_col:]
    own_ref, send_ref, terms_ref, buf, table, picked, select, part, sems, *acc = refs
    kvec, own = gath[0].shape
    slots = tiles.shape[0]
    blk_own = own // side
    per = LANES // side
    n_chunk = tiles.shape[1] // LANES
    count = count_s[0]
    my_row = lax.axis_index("row")
    my_col = lax.axis_index("col")

    def tile_copy(ch):
        span = pl.ds(pl.multiple_of(ch * CHUNK, CHUNK), CHUNK)
        return pltpu.make_async_copy(tiles.at[span], buf.at[span], sems.at[ch])

    used = (count + CHUNK - 1) // CHUNK

    def start(ch, carry):
        tile_copy(ch).start()
        return carry

    lax.fori_loop(0, used, start, 0)

    lane = lax.broadcasted_iota(jnp.int32, (kvec, LANES), 1)
    low = lane < side
    zero = jnp.zeros((kvec, LANES), jnp.float32)

    for s in range(n_row):
        first = lax.rem(my_row + (n_row - s), n_row) * blk_own
        for p in range(own // LANES):
            x = gath[s][:, p * LANES:(p + 1) * LANES].astype(jnp.float32)
            y = pltpu.roll(x, side, 1)
            at = first + p * per
            even = jnp.concatenate([jnp.where(low, x, zero), jnp.where(low, zero, y)], axis=0)
            odd = jnp.concatenate([jnp.where(low, y, zero), jnp.where(low, zero, x)], axis=0)
            table[at] = even.astype(jnp.bfloat16)
            table[at + 1] = odd.astype(jnp.bfloat16)
    n_blocks = n_row * blk_own
    table[n_blocks] = jnp.zeros((per * kvec, LANES), jnp.bfloat16)

    n_seg = acc[0].shape[0]
    width = n_chunk * SUB
    depth = per * per * width

    def clear(r, carry):
        for a in acc:
            a[r] = jnp.zeros(a.shape[1:], jnp.float32)
        return carry

    lax.fori_loop(0, n_seg, clear, 0)

    k_id = lax.broadcasted_iota(jnp.int32, (width, LANES), 0)
    n_id = lax.broadcasted_iota(jnp.int32, (width, LANES), 1)
    base_id = n_id - per * (k_id // SUB)
    for par in range(per):
        for jp in range(per):
            at = (par * per + jp) * width
            hit = (base_id == side * par + jp).astype(jnp.float32)
            select[at:at + width, :] = hit.astype(jnp.bfloat16)

    rows_of = per * kvec

    def product(base, half, x):
        xh = x[half * SUB:(half + 1) * SUB]
        w = jnp.concatenate(
            [xh[:, c * LANES:(c + 1) * LANES] for c in range(n_chunk)], axis=0
        ).astype(jnp.bfloat16)
        entries = []
        for t in range(SUB):
            slot = base + half * SUB + t
            entries.append(table[jnp.where(slot < count, cols_s[slot], n_blocks)])
        left = jnp.concatenate(entries, axis=0)
        return lax.dot_general(left, w, NT, preferred_element_type=jnp.float32)

    def accumulate(at, out):
        for t in range(SUB):
            r = rows_s[at + t]
            acc[t][r] += out[t * rows_of:(t + 1) * rows_of]

    def one_chunk(ch, carry):
        tile_copy(ch).wait()
        waiting = None
        for q in range(CHUNK // (2 * SUB)):
            base = pl.multiple_of(ch * CHUNK + q * 2 * SUB, 2 * SUB)
            x = buf[pl.ds(base, 2 * SUB), :].astype(jnp.float32)
            for half in range(2):
                out = product(base, half, x)
                if waiting is not None:
                    accumulate(*waiting)
                waiting = (base + half * SUB, out)
        accumulate(*waiting)
        return carry

    lax.fori_loop(0, used, one_chunk, 0)

    lane_w = lax.broadcasted_iota(jnp.int32, (rows_of, width), 1) % SUB
    pairs = n_seg // per

    def pick(m, carry):
        pieces = []
        for par in range(per):
            total = jnp.zeros((rows_of, width), jnp.float32)
            for t in range(SUB):
                total = jnp.where(lane_w == t, acc[t][m * per + par], total)
            for jp in range(per):
                pieces.append(total[jp * kvec:(jp + 1) * kvec])
        a = jnp.concatenate(pieces, axis=1)
        hi = a.astype(jnp.bfloat16).astype(jnp.float32)
        both = jnp.concatenate([hi, a - hi], axis=0).astype(jnp.bfloat16)
        picked[pl.ds(pl.multiple_of(m * 2 * kvec, 2 * kvec), 2 * kvec), :] = both
        return carry

    lax.fori_loop(0, pairs, pick, 0)

    spread = jnp.dot(picked[...], select[...], preferred_element_type=jnp.float32)
    for m in range(pairs):
        at = m * 2 * kvec
        row = spread[at:at + kvec] + spread[at + kvec:at + 2 * kvec]
        c, lane0 = divmod(m * LANES, own)
        part[c, :, lane0:lane0 + LANES] = row

    part[my_col] += ener[...] * seg[0][...].astype(jnp.float32)
    own_ref[...] = part[my_col]
    terms = jnp.zeros((kvec, kvec), jnp.float32)
    for s in range(n_col):
        share = part[lax.rem(my_col + s, n_col)]
        if s > 0:
            send_ref[s - 1] = share.astype(jnp.bfloat16)
        terms = terms + lax.dot_general(
            seg[(n_col - s) % n_col][...].astype(jnp.float32), share, NT,
            precision=lax.Precision.HIGHEST, preferred_element_type=jnp.float32,
        )
    terms_ref[...] = terms


def tile_work(rows, cols, count, gath, seg, ener, tiles):
    n_row, n_col = len(gath), len(seg)
    kvec, own = gath[0].shape
    slots, area = tiles.shape
    side = math.isqrt(area)
    per = LANES // side
    blk_own = own // side
    n_seg = n_col * blk_own
    width = area // LANES * SUB
    vmem = pl.BlockSpec(memory_space=pltpu.VMEM)
    smem = pl.BlockSpec(memory_space=pltpu.SMEM)
    return pl.pallas_call(
        functools.partial(tile_kernel, n_row, n_col, side),
        out_shape=(
            jax.ShapeDtypeStruct((kvec, own), jnp.float32),
            jax.ShapeDtypeStruct((n_col - 1, kvec, own), jnp.bfloat16),
            jax.ShapeDtypeStruct((kvec, kvec), jnp.float32),
        ),
        in_specs=[smem, smem, smem, vmem, pl.BlockSpec(memory_space=pl.ANY)]
        + [vmem] * (n_row + n_col),
        out_specs=(vmem, vmem, vmem),
        scratch_shapes=[
            pltpu.VMEM((slots, area), jnp.bfloat16),
            pltpu.VMEM((n_row * blk_own + 1, per * kvec, LANES), jnp.bfloat16),
            pltpu.VMEM((n_seg // per * 2 * kvec, per * per * width), jnp.bfloat16),
            pltpu.VMEM((per * per * width, LANES), jnp.bfloat16),
            pltpu.VMEM((n_col, kvec, own), jnp.float32),
            pltpu.SemaphoreType.DMA((slots // CHUNK,)),
        ] + [pltpu.VMEM((n_seg, per * kvec, width), jnp.float32)] * SUB,
        compiler_params=pltpu.CompilerParams(vmem_limit_bytes=48 * 2**20),
        cost_estimate=pl.CostEstimate(
            flops=2 * slots * area * kvec, bytes_accessed=2 * slots * area, transcendentals=0
        ),
        name="tile_work",
    )(rows, cols, count, ener, tiles, *gath, *seg)


def from_all(x, axes, size, group, stride):
    got = [x]
    for s in range(1, group):
        perm = []
        for i in range(size):
            place = i // stride % group
            perm.append((i, i + ((place + s) % group - place) * stride))
        got.append(lax.ppermute(x, axes, perm))
    return got


def sum_everywhere(x, axes, size):
    stride = 1
    while stride < size:
        group = math.gcd(size // stride, WIDEST)
        if group == 1:
            group = size // stride
        x = sum(from_all(x, axes, size, group, stride))
        stride *= group
    return x


def per_device(vectors, energies, tiles, tile_rows, tile_cols, tile_count):
    kvec, own = vectors.shape
    n_row = lax.axis_size("row")
    n_col = lax.axis_size("col")
    seg = from_all(vectors, "col", n_col, n_col, 1)
    gath = from_all(vectors, "row", n_row, n_row, 1)
    base, send, terms = tile_work(
        tile_rows, tile_cols, tile_count, gath, seg, energies[None, :], tiles
    )
    whole = base
    for s in range(1, n_col):
        got = lax.ppermute(send[s - 1], "col", [(c, (c + s) % n_col) for c in range(n_col)])
        whole = whole + got.astype(jnp.float32)
    gram = sum_everywhere(terms, ("row", "col"), n_row * n_col) / (n_row * n_col * own)
    vec32 = vectors.astype(jnp.float32)
    residual = whole - jnp.einsum("ab,an->bn", gram, vec32, precision=lax.Precision.HIGHEST)
    return (whole.astype(jnp.bfloat16), residual)


def solution(mesh):
    in_specs = (
        P(None, ("row", "col")),
        P(("row", "col")),
        P(("row", "col"), None),
        P(("row", "col")),
        P(("row", "col")),
        P(("row", "col")),
    )
    out_specs = (P(None, ("row", "col")), P(None, ("row", "col")))
    return jax.shard_map(
        per_device, mesh=mesh, in_specs=in_specs, out_specs=out_specs, check_vma=False
    )
```

time: 61.9 us -> 93.6 us (1.51); the launches traced: 61.6 us -> 92.2 us
  starting transfers between devices: 7.75 us -> 65.9 us
  blocking collectives: 28.6 us -> 0 us
  waiting for transfers between devices: 11.3 us -> 16.3 us
  Pallas kernels: 9.04 us -> 4.43 us
  local copies, waits for them, and re-layouts: 1.38 us -> 2.78 us
    ppermute x5 -> x47, starting transfers between devices: 6.96 us -> 65.8 us  [from_all(): got.append(lax.ppermute(x, axes, perm))]
    all_gather x2 -> x0, blocking collectives: 28.6 us -> none  [the longest x1 23 us: per_device(): gath = lax.all_gather(vectors, 'row', axis=0)]
    ppermute x5 -> x47, waiting for transfers between devices: 11.3 us -> 16.3 us  [from_all(): got.append(lax.ppermute(x, axes, perm))]
    pallas_call x1, Pallas kernels: 9.04 us -> 4.43 us  [tile_work(): pl.pallas_call(functools.partial(tile_kernel, n_row, n_col, side), out_sh...]
    unnamed x6 -> x8, local copies, waits for them, and re-layouts: 1.38 us -> 2.78 us
  transfers between devices with their start and end apart: 6 -> 48, of which waited for: 5 -> 11; matrix products, arithmetic and copies ran while one was open for 1% -> 1% of each run, Pallas kernels for 0% -> 0%
where the time goes in v2:
time: 93.6 us; the launch traced here: 92.2 us
  starting transfers between devices  65.9 us (70%)
  waiting for transfers between devices  16.3 us (17%)
  Pallas kernels  4.43 us (5%)
  local copies, waits for them, and re-layouts  2.78 us (3%)
  between operations  1.37 us (1%)
    ppermute x47, starting transfers between devices, from_all(): got.append(lax.ppermute(x, axes, perm))  65.8 us
    ppermute x47, waiting for transfers between devices, from_all(): got.append(lax.ppermute(x, axes, perm))  16.3 us
    pallas_call x1, Pallas kernels, tile_work(): pl.pallas_call(functools.partial(tile_kernel, n_row, n_col, side), out_sh...  4.43 us
    unnamed x8, local copies, waits for them, and re-layouts  2.78 us
  transfers between devices with their start and end apart: 48, of which 11 were waited for; matrix products, arithmetic and copies ran while one was open for 1% of the time, Pallas kernels for 0%

profile of v2, /device:TPU:0, one launch (start us, length us, event | category | flops | bytes accessed | tf_op | source)
XLA Modules:
  0.0 92.2 jit_solution(13537377109722089783)
XLA Ops:
  0.6 3.0 %collective-permute-start.15 = (bf16[8,1024]{1,0:T(8,128)(2,1)}, bf16[8,1024]{1,0:T(8,128)(2,1)S(1)}, u32[]{:S(2)}, u32[]{:S(2)}) collective-permute-start(bf16[8,1024]{1,0:T(8,128)(2,1)} %refs_16_.1), channel_id=1, source_target_pairs={{0,1},{1,0},{2,3},{3,2},{4,5},{5,4},{6,7},{7,6},{8,9},{9,8},{10,11... | collective-permute-start | bytes 49160 | tf_op jit(solution)/shard_map/ppermute | solution.py:202
  3.7 3.7 %collective-permute-start.14 = (bf16[8,1024]{1,0:T(8,128)(2,1)}, bf16[8,1024]{1,0:T(8,128)(2,1)S(1)}, u32[]{:S(2)}, u32[]{:S(2)}) collective-permute-start(bf16[8,1024]{1,0:T(8,128)(2,1)} %refs_16_.1), channel_id=1, source_target_pairs={{0,30},{2,0},{4,2},{6,4},{8,6},{10,8},{12,10},{14,12},{16,14},{18,... | collective-permute-start | bytes 49160 | tf_op jit(solution)/shard_map/ppermute | solution.py:202
  9.0 4.1 %collective-permute-start.9 = (bf16[8,1024]{1,0:T(8,128)(2,1)}, bf16[8,1024]{1,0:T(8,128)(2,1)S(1)}, u32[]{:S(2)}, u32[]{:S(2)}) collective-permute-start(bf16[8,1024]{1,0:T(8,128)(2,1)} %refs_16_.1), channel_id=1, source_target_pairs={{0,20},{2,22},{4,24},{6,26},{8,28},{10,30},{12,0},{14,2},{16,4},{1... | collective-permute-start | bytes 49160 | tf_op jit(solution)/shard_map/ppermute | solution.py:202
  13.1 1.6 %collective-permute-start.7 = (bf16[8,1024]{1,0:T(8,128)(2,1)}, bf16[8,1024]{1,0:T(8,128)(2,1)S(1)}, u32[]{:S(2)}, u32[]{:S(2)}) collective-permute-start(bf16[8,1024]{1,0:T(8,128)(2,1)} %refs_16_.1), channel_id=1, source_target_pairs={{0,16},{2,18},{4,20},{6,22},{8,24},{10,26},{12,28},{14,30},{16,0},... | collective-permute-start | bytes 49160 | tf_op jit(solution)/shard_map/ppermute | solution.py:202
  14.7 1.1 %collective-permute-start.6 = (bf16[8,1024]{1,0:T(8,128)(2,1)}, bf16[8,1024]{1,0:T(8,128)(2,1)S(1)}, u32[]{:S(2)}, u32[]{:S(2)}) collective-permute-start(bf16[8,1024]{1,0:T(8,128)(2,1)} %refs_16_.1), channel_id=1, source_target_pairs={{0,14},{2,16},{4,18},{6,20},{8,22},{10,24},{12,26},{14,28},{16,30}... | collective-permute-start | bytes 49160 | tf_op jit(solution)/shard_map/ppermute | solution.py:202
  15.8 2.9 %collective-permute-start.5 = (bf16[8,1024]{1,0:T(8,128)(2,1)}, bf16[8,1024]{1,0:T(8,128)(2,1)S(1)}, u32[]{:S(2)}, u32[]{:S(2)}) collective-permute-start(bf16[8,1024]{1,0:T(8,128)(2,1)} %refs_16_.1), channel_id=1, source_target_pairs={{0,12},{2,14},{4,16},{6,18},{8,20},{10,22},{12,24},{14,26},{16,28}... | collective-permute-start | bytes 49160 | tf_op jit(solution)/shard_map/ppermute | solution.py:202
  19.2 2.0 %collective-permute-start.3 = (bf16[8,1024]{1,0:T(8,128)(2,1)}, bf16[8,1024]{1,0:T(8,128)(2,1)S(1)}, u32[]{:S(2)}, u32[]{:S(2)}) collective-permute-start(bf16[8,1024]{1,0:T(8,128)(2,1)} %refs_16_.1), channel_id=1, source_target_pairs={{0,8},{2,10},{4,12},{6,14},{8,16},{10,18},{12,20},{14,22},{16,24},... | collective-permute-start | bytes 49160 | tf_op jit(solution)/shard_map/ppermute | solution.py:202
  21.2 2.1 %collective-permute-start.2 = (bf16[8,1024]{1,0:T(8,128)(2,1)}, bf16[8,1024]{1,0:T(8,128)(2,1)S(1)}, u32[]{:S(2)}, u32[]{:S(2)}) collective-permute-start(bf16[8,1024]{1,0:T(8,128)(2,1)} %refs_16_.1), channel_id=1, source_target_pairs={{0,6},{2,8},{4,10},{6,12},{8,14},{10,16},{12,18},{14,20},{16,22},{... | collective-permute-start | bytes 49160 | tf_op jit(solution)/shard_map/ppermute | solution.py:202
  25.0 1.9 %collective-permute-done.2.refs_3_ = bf16[8,1024]{1,0:T(8,128)(2,1)S(1)} collective-permute-done((bf16[8,1024]{1,0:T(8,128)(2,1)}, bf16[8,1024]{1,0:T(8,128)(2,1)S(1)}, u32[]{:S(2)}, u32[]{:S(2)}) %collective-permute-start.2) | collective-permute-done | bytes 16416 | tf_op jit(solution)/shard_map/ppermute | solution.py:202
  26.9 3.1 %collective-permute-done.1.refs_2_ = bf16[8,1024]{1,0:T(8,128)(2,1)S(1)} collective-permute-done((bf16[8,1024]{1,0:T(8,128)(2,1)}, bf16[8,1024]{1,0:T(8,128)(2,1)S(1)}, u32[]{:S(2)}, u32[]{:S(2)}) %collective-permute-start.1) | collective-permute-done | bytes 16416 | tf_op jit(solution)/shard_map/ppermute | solution.py:202
  32.7 4.4 %tile_work.1 = (f32[8,1024]{1,0:T(8,128)S(1)}, bf16[1,8,1024]{2,1,0:T(8,128)(2,1)S(1)}, f32[8,8]{1,0:T(8,128)S(1)}) custom-call(s32[1024]{0:T(1024)S(1)} %copy-done.1, s32[1024]{0:T(1024)S(1)} %copy-done.2, s32[1]{0:T(128)S(6)} %copy.8.count_s, f32[1,1024]{1,0:T(1,128)S(1)} %bitcast.3, bf16[1024,4096]{1,0:T(8,128)(2,1)} %tiles.1, ...), custom_call_target="tpu_custom_call" | custom-call | flops 67108864 | bytes 8388608 | tf_op jit(solution)/shard_map/tile_work/pallas_call | solution.py:169
  37.6 2.2 %collective-permute-start.46 = (f32[8,8]{1,0:T(8,128)S(1)}, f32[8,8]{1,0:T(8,128)S(1)}, u32[]{:S(2)}, u32[]{:S(2)}) collective-permute-start(f32[8,8]{1,0:T(8,128)S(1)} %get-tuple-element.7), channel_id=1, source_target_pairs={{0,30},{1,31},{2,0},{3,1},{4,2},{5,3},{6,4},{7,5},{8,6},{9,7},{10,... | collective-permute-start | bytes 776 | tf_op jit(solution)/shard_map/ppermute | solution.py:202
  40.5 4.9 %collective-permute-start.44 = (f32[8,8]{1,0:T(8,128)S(1)}, f32[8,8]{1,0:T(8,128)S(1)}, u32[]{:S(2)}, u32[]{:S(2)}) collective-permute-start(f32[8,8]{1,0:T(8,128)S(1)} %get-tuple-element.7), channel_id=1, source_target_pairs={{0,28},{1,29},{2,30},{3,31},{4,0},{5,1},{6,2},{7,3},{8,4},{9,5},{1... | collective-permute-start | bytes 776 | tf_op jit(solution)/shard_map/ppermute | solution.py:202
  45.6 2.8 %collective-permute-start.41 = (f32[8,8]{1,0:T(8,128)S(1)}, f32[8,8]{1,0:T(8,128)S(1)}, u32[]{:S(2)}, u32[]{:S(2)}) collective-permute-start(f32[8,8]{1,0:T(8,128)S(1)} %get-tuple-element.7), channel_id=1, source_target_pairs={{0,25},{1,26},{2,27},{3,28},{4,29},{5,30},{6,31},{7,0},{8,1},{9,2}... | collective-permute-start | bytes 776 | tf_op jit(solution)/shard_map/ppermute | solution.py:202
  48.4 1.5 %collective-permute-done.43 = f32[8,8]{1,0:T(8,128)S(1)} collective-permute-done((f32[8,8]{1,0:T(8,128)S(1)}, f32[8,8]{1,0:T(8,128)S(1)}, u32[]{:S(2)}, u32[]{:S(2)}) %collective-permute-start.43) | collective-permute-done | bytes 288 | tf_op jit(solution)/shard_map/ppermute | solution.py:202
  50.4 2.2 %collective-permute-start.38 = (f32[8,8]{1,0:T(8,128)S(1)}, f32[8,8]{1,0:T(8,128)S(1)}, u32[]{:S(2)}, u32[]{:S(2)}) collective-permute-start(f32[8,8]{1,0:T(8,128)S(1)} %get-tuple-element.7), channel_id=1, source_target_pairs={{0,22},{1,23},{2,24},{3,25},{4,26},{5,27},{6,28},{7,29},{8,30},{9,... | collective-permute-start | bytes 776 | tf_op jit(solution)/shard_map/ppermute | solution.py:202
  52.6 1.2 %collective-permute-start.37 = (f32[8,8]{1,0:T(8,128)S(1)}, f32[8,8]{1,0:T(8,128)S(1)}, u32[]{:S(2)}, u32[]{:S(2)}) collective-permute-start(f32[8,8]{1,0:T(8,128)S(1)} %get-tuple-element.7), channel_id=1, source_target_pairs={{0,21},{1,22},{2,23},{3,24},{4,25},{5,26},{6,27},{7,28},{8,29},{9,... | collective-permute-start | bytes 776 | tf_op jit(solution)/shard_map/ppermute | solution.py:202
  53.9 1.7 %collective-permute-start.36 = (f32[8,8]{1,0:T(8,128)S(1)}, f32[8,8]{1,0:T(8,128)S(1)}, u32[]{:S(2)}, u32[]{:S(2)}) collective-permute-start(f32[8,8]{1,0:T(8,128)S(1)} %get-tuple-element.7), channel_id=1, source_target_pairs={{0,20},{1,21},{2,22},{3,23},{4,24},{5,25},{6,26},{7,27},{8,28},{9,... | collective-permute-start | bytes 776 | tf_op jit(solution)/shard_map/ppermute | solution.py:202
  55.5 2.9 %collective-permute-start.35 = (f32[8,8]{1,0:T(8,128)S(1)}, f32[8,8]{1,0:T(8,128)S(1)}, u32[]{:S(2)}, u32[]{:S(2)}) collective-permute-start(f32[8,8]{1,0:T(8,128)S(1)} %get-tuple-element.7), channel_id=1, source_target_pairs={{0,19},{1,20},{2,21},{3,22},{4,23},{5,24},{6,25},{7,26},{8,27},{9,... | collective-permute-start | bytes 776 | tf_op jit(solution)/shard_map/ppermute | solution.py:202
  58.4 2.6 %collective-permute-start.34 = (f32[8,8]{1,0:T(8,128)S(1)}, f32[8,8]{1,0:T(8,128)S(1)}, u32[]{:S(2)}, u32[]{:S(2)}) collective-permute-start(f32[8,8]{1,0:T(8,128)S(1)} %get-tuple-element.7), channel_id=1, source_target_pairs={{0,18},{1,19},{2,20},{3,21},{4,22},{5,23},{6,24},{7,25},{8,26},{9,... | collective-permute-start | bytes 776 | tf_op jit(solution)/shard_map/ppermute | solution.py:202
  61.0 1.6 %collective-permute-start.33 = (f32[8,8]{1,0:T(8,128)S(1)}, f32[8,8]{1,0:T(8,128)S(1)}, u32[]{:S(2)}, u32[]{:S(2)}) collective-permute-start(f32[8,8]{1,0:T(8,128)S(1)} %get-tuple-element.7), channel_id=1, source_target_pairs={{0,17},{1,18},{2,19},{3,20},{4,21},{5,22},{6,23},{7,24},{8,25},{9,... | collective-permute-start | bytes 776 | tf_op jit(solution)/shard_map/ppermute | solution.py:202
  62.6 1.8 %collective-permute-start.32 = (f32[8,8]{1,0:T(8,128)S(1)}, f32[8,8]{1,0:T(8,128)S(1)}, u32[]{:S(2)}, u32[]{:S(2)}) collective-permute-start(f32[8,8]{1,0:T(8,128)S(1)} %get-tuple-element.7), channel_id=1, source_target_pairs={{0,16},{1,17},{2,18},{3,19},{4,20},{5,21},{6,22},{7,23},{8,24},{9,... | collective-permute-start | bytes 776 | tf_op jit(solution)/shard_map/ppermute | solution.py:202
  65.9 3.5 %collective-permute-start.29 = (f32[8,8]{1,0:T(8,128)S(1)}, f32[8,8]{1,0:T(8,128)S(1)}, u32[]{:S(2)}, u32[]{:S(2)}) collective-permute-start(f32[8,8]{1,0:T(8,128)S(1)} %get-tuple-element.7), channel_id=1, source_target_pairs={{0,13},{1,14},{2,15},{3,16},{4,17},{5,18},{6,19},{7,20},{8,21},{9,... | collective-permute-start | bytes 776 | tf_op jit(solution)/shard_map/ppermute | solution.py:202
  69.3 1.9 %collective-permute-start.28 = (f32[8,8]{1,0:T(8,128)S(1)}, f32[8,8]{1,0:T(8,128)S(1)}, u32[]{:S(2)}, u32[]{:S(2)}) collective-permute-start(f32[8,8]{1,0:T(8,128)S(1)} %get-tuple-element.7), channel_id=1, source_target_pairs={{0,12},{1,13},{2,14},{3,15},{4,16},{5,17},{6,18},{7,19},{8,20},{9,... | collective-permute-start | bytes 776 | tf_op jit(solution)/shard_map/ppermute | solution.py:202
  71.3 1.9 %collective-permute-start.26 = (f32[8,8]{1,0:T(8,128)S(1)}, f32[8,8]{1,0:T(8,128)S(1)}, u32[]{:S(2)}, u32[]{:S(2)}) collective-permute-start(f32[8,8]{1,0:T(8,128)S(1)} %get-tuple-element.7), channel_id=1, source_target_pairs={{0,10},{1,11},{2,12},{3,13},{4,14},{5,15},{6,16},{7,17},{8,18},{9,... | collective-permute-start | bytes 776 | tf_op jit(solution)/shard_map/ppermute | solution.py:202
  73.1 1.6 %collective-permute-start.25 = (f32[8,8]{1,0:T(8,128)S(1)}, f32[8,8]{1,0:T(8,128)S(1)}, u32[]{:S(2)}, u32[]{:S(2)}) collective-permute-start(f32[8,8]{1,0:T(8,128)S(1)} %get-tuple-element.7), channel_id=1, source_target_pairs={{0,9},{1,10},{2,11},{3,12},{4,13},{5,14},{6,15},{7,16},{8,17},{9,1... | collective-permute-start | bytes 776 | tf_op jit(solution)/shard_map/ppermute | solution.py:202
  75.7 1.8 %collective-permute-done.27 = f32[8,8]{1,0:T(8,128)S(1)} collective-permute-done((f32[8,8]{1,0:T(8,128)S(1)}, f32[8,8]{1,0:T(8,128)S(1)}, u32[]{:S(2)}, u32[]{:S(2)}) %collective-permute-start.27) | collective-permute-done | bytes 288 | tf_op jit(solution)/shard_map/ppermute | solution.py:202
  78.9 3.3 %collective-permute-start.21 = (f32[8,8]{1,0:T(8,128)S(1)}, f32[8,8]{1,0:T(8,128)S(1)}, u32[]{:S(2)}, u32[]{:S(2)}) collective-permute-start(f32[8,8]{1,0:T(8,128)S(1)} %get-tuple-element.7), channel_id=1, source_target_pairs={{0,5},{1,6},{2,7},{3,8},{4,9},{5,10},{6,11},{7,12},{8,13},{9,14},{... | collective-permute-start | bytes 776 | tf_op jit(solution)/shard_map/ppermute | solution.py:202
  82.2 1.6 %collective-permute-done.23 = f32[8,8]{1,0:T(8,128)S(1)} collective-permute-done((f32[8,8]{1,0:T(8,128)S(1)}, f32[8,8]{1,0:T(8,128)S(1)}, u32[]{:S(2)}, u32[]{:S(2)}) %collective-permute-start.23) | collective-permute-done | bytes 288 | tf_op jit(solution)/shard_map/ppermute | solution.py:202
  84.0 2.2 %collective-permute-start.17 = (f32[8,8]{1,0:T(8,128)S(1)}, f32[8,8]{1,0:T(8,128)S(1)}, u32[]{:S(2)}, u32[]{:S(2)}) collective-permute-start(f32[8,8]{1,0:T(8,128)S(1)} %get-tuple-element.7), channel_id=1, source_target_pairs={{0,1},{1,2},{2,3},{3,4},{4,5},{5,6},{6,7},{7,8},{8,9},{9,10},{10,1... | collective-permute-start | bytes 776 | tf_op jit(solution)/shard_map/ppermute | solution.py:202
  86.8 1.7 %collective-permute-done.20 = f32[8,8]{1,0:T(8,128)S(1)} collective-permute-done((f32[8,8]{1,0:T(8,128)S(1)}, f32[8,8]{1,0:T(8,128)S(1)}, u32[]{:S(2)}, u32[]{:S(2)}) %collective-permute-start.20) | collective-permute-done | bytes 288 | tf_op jit(solution)/shard_map/ppermute | solution.py:202
  88.5 2.5 %collective-permute-done.19 = f32[8,8]{1,0:T(8,128)S(1)} collective-permute-done((f32[8,8]{1,0:T(8,128)S(1)}, f32[8,8]{1,0:T(8,128)S(1)}, u32[]{:S(2)}, u32[]{:S(2)}) %collective-permute-start.19) | collective-permute-done | bytes 288 | tf_op jit(solution)/shard_map/ppermute | solution.py:202
  (75 shorter events, 13.6 us)
Async XLA Ops:
  0.6 8.3 %collective-permute-start.15 = (bf16[8,1024]{1,0:T(8,128)(2,1)}, bf16[8,1024]{1,0:T(8,128)(2,1)S(1)}, u32[]{:S(2)}, u32[]{:S(2)}) collective-permute-start(bf16[8,1024]{1,0:T(8,128)(2,1)} %refs_16_.1), channel_id=1, source_target_pairs={{0,1},{1,0},{2,3},{3,2},{4,5},{5,4},{6,7},{7,6},{8,9},{9,8},{10,11... | collective-permute-start | bytes 49160 | tf_op jit(solution)/shard_map/ppermute | solution.py:202
  8.5 6.2 %collective-permute-start.11 = (bf16[8,1024]{1,0:T(8,128)(2,1)}, bf16[8,1024]{1,0:T(8,128)(2,1)S(1)}, u32[]{:S(2)}, u32[]{:S(2)}) collective-permute-start(bf16[8,1024]{1,0:T(8,128)(2,1)} %refs_16_.1), channel_id=1, source_target_pairs={{0,24},{2,26},{4,28},{6,30},{8,0},{10,2},{12,4},{14,6},{16,8},{18,... | collective-permute-start | bytes 49160 | tf_op jit(solution)/shard_map/ppermute | solution.py:202
  8.9 6.9 %collective-permute-start.10 = (bf16[8,1024]{1,0:T(8,128)(2,1)}, bf16[8,1024]{1,0:T(8,128)(2,1)S(1)}, u32[]{:S(2)}, u32[]{:S(2)}) collective-permute-start(bf16[8,1024]{1,0:T(8,128)(2,1)} %refs_16_.1), channel_id=1, source_target_pairs={{0,22},{2,24},{4,26},{6,28},{8,30},{10,0},{12,2},{14,4},{16,6},{18... | collective-permute-start | bytes 49160 | tf_op jit(solution)/shard_map/ppermute | solution.py:202
  9.0 9.7 %collective-permute-start.9 = (bf16[8,1024]{1,0:T(8,128)(2,1)}, bf16[8,1024]{1,0:T(8,128)(2,1)S(1)}, u32[]{:S(2)}, u32[]{:S(2)}) collective-permute-start(bf16[8,1024]{1,0:T(8,128)(2,1)} %refs_16_.1), channel_id=1, source_target_pairs={{0,20},{2,22},{4,24},{6,26},{8,28},{10,30},{12,0},{14,2},{16,4},{1... | collective-permute-start | bytes 49160 | tf_op jit(solution)/shard_map/ppermute | solution.py:202
  13.1 8.1 %collective-permute-start.7 = (bf16[8,1024]{1,0:T(8,128)(2,1)}, bf16[8,1024]{1,0:T(8,128)(2,1)S(1)}, u32[]{:S(2)}, u32[]{:S(2)}) collective-permute-start(bf16[8,1024]{1,0:T(8,128)(2,1)} %refs_16_.1), channel_id=1, source_target_pairs={{0,16},{2,18},{4,20},{6,22},{8,24},{10,26},{12,28},{14,30},{16,0},... | collective-permute-start | bytes 49160 | tf_op jit(solution)/shard_map/ppermute | solution.py:202
  14.7 8.6 %collective-permute-start.6 = (bf16[8,1024]{1,0:T(8,128)(2,1)}, bf16[8,1024]{1,0:T(8,128)(2,1)S(1)}, u32[]{:S(2)}, u32[]{:S(2)}) collective-permute-start(bf16[8,1024]{1,0:T(8,128)(2,1)} %refs_16_.1), channel_id=1, source_target_pairs={{0,14},{2,16},{4,18},{6,20},{8,22},{10,24},{12,26},{14,28},{16,30}... | collective-permute-start | bytes 49160 | tf_op jit(solution)/shard_map/ppermute | solution.py:202
  15.8 7.8 %collective-permute-start.5 = (bf16[8,1024]{1,0:T(8,128)(2,1)}, bf16[8,1024]{1,0:T(8,128)(2,1)S(1)}, u32[]{:S(2)}, u32[]{:S(2)}) collective-permute-start(bf16[8,1024]{1,0:T(8,128)(2,1)} %refs_16_.1), channel_id=1, source_target_pairs={{0,12},{2,14},{4,16},{6,18},{8,20},{10,22},{12,24},{14,26},{16,28}... | collective-permute-start | bytes 49160 | tf_op jit(solution)/shard_map/ppermute | solution.py:202
  23.3 6.6 %collective-permute-start.1 = (bf16[8,1024]{1,0:T(8,128)(2,1)}, bf16[8,1024]{1,0:T(8,128)(2,1)S(1)}, u32[]{:S(2)}, u32[]{:S(2)}) collective-permute-start(bf16[8,1024]{1,0:T(8,128)(2,1)} %refs_16_.1), channel_id=1, source_target_pairs={{0,4},{2,6},{4,8},{6,10},{8,12},{10,14},{12,16},{14,18},{16,20},{1... | collective-permute-start | bytes 49160 | tf_op jit(solution)/shard_map/ppermute | solution.py:202
  23.6 6.4 %collective-permute-start = (bf16[8,1024]{1,0:T(8,128)(2,1)}, bf16[8,1024]{1,0:T(8,128)(2,1)S(1)}, u32[]{:S(2)}, u32[]{:S(2)}) collective-permute-start(bf16[8,1024]{1,0:T(8,128)(2,1)} %refs_16_.1), channel_id=1, source_target_pairs={{0,2},{2,4},{4,6},{6,8},{8,10},{10,12},{12,14},{14,16},{16,18},{18... | collective-permute-start | bytes 49160 | tf_op jit(solution)/shard_map/ppermute | solution.py:202
  37.2 46.8 %collective-permute-start.16 = (bf16[8,1024]{1,0:T(8,128)(2,1)S(1)}, bf16[8,1024]{1,0:T(8,128)(2,1)S(1)}, u32[]{:S(2)}, u32[]{:S(2)}) collective-permute-start(bf16[8,1024]{1,0:T(8,128)(2,1)S(1)} %bitcast.4), channel_id=1, source_target_pairs={{0,1},{1,0},{2,3},{3,2},{4,5},{5,4},{6,7},{7,6},{8,9},{9,8},{10,11... | collective-permute-start | bytes 49160 | tf_op jit(solution)/shard_map/ppermute | solution.py:228
  37.3 8.1 %collective-permute-start.47 = (f32[8,8]{1,0:T(8,128)S(1)}, f32[8,8]{1,0:T(8,128)S(1)}, u32[]{:S(2)}, u32[]{:S(2)}) collective-permute-start(f32[8,8]{1,0:T(8,128)S(1)} %get-tuple-element.7), channel_id=1, source_target_pairs={{0,31},{1,0},{2,1},{3,2},{4,3},{5,4},{6,5},{7,6},{8,7},{9,8},{10,9... | collective-permute-start | bytes 776 | tf_op jit(solution)/shard_map/ppermute | solution.py:202
  37.6 7.8 %collective-permute-start.46 = (f32[8,8]{1,0:T(8,128)S(1)}, f32[8,8]{1,0:T(8,128)S(1)}, u32[]{:S(2)}, u32[]{:S(2)}) collective-permute-start(f32[8,8]{1,0:T(8,128)S(1)} %get-tuple-element.7), channel_id=1, source_target_pairs={{0,30},{1,31},{2,0},{3,1},{4,2},{5,3},{6,4},{7,5},{8,6},{9,7},{10,... | collective-permute-start | bytes 776 | tf_op jit(solution)/shard_map/ppermute | solution.py:202
  40.5 7.9 %collective-permute-start.44 = (f32[8,8]{1,0:T(8,128)S(1)}, f32[8,8]{1,0:T(8,128)S(1)}, u32[]{:S(2)}, u32[]{:S(2)}) collective-permute-start(f32[8,8]{1,0:T(8,128)S(1)} %get-tuple-element.7), channel_id=1, source_target_pairs={{0,28},{1,29},{2,30},{3,31},{4,0},{5,1},{6,2},{7,3},{8,4},{9,5},{1... | collective-permute-start | bytes 776 | tf_op jit(solution)/shard_map/ppermute | solution.py:202
  45.6 7.0 %collective-permute-start.41 = (f32[8,8]{1,0:T(8,128)S(1)}, f32[8,8]{1,0:T(8,128)S(1)}, u32[]{:S(2)}, u32[]{:S(2)}) collective-permute-start(f32[8,8]{1,0:T(8,128)S(1)} %get-tuple-element.7), channel_id=1, source_target_pairs={{0,25},{1,26},{2,27},{3,28},{4,29},{5,30},{6,31},{7,0},{8,1},{9,2}... | collective-permute-start | bytes 776 | tf_op jit(solution)/shard_map/ppermute | solution.py:202
  50.4 8.0 %collective-permute-start.38 = (f32[8,8]{1,0:T(8,128)S(1)}, f32[8,8]{1,0:T(8,128)S(1)}, u32[]{:S(2)}, u32[]{:S(2)}) collective-permute-start(f32[8,8]{1,0:T(8,128)S(1)} %get-tuple-element.7), channel_id=1, source_target_pairs={{0,22},{1,23},{2,24},{3,25},{4,26},{5,27},{6,28},{7,29},{8,30},{9,... | collective-permute-start | bytes 776 | tf_op jit(solution)/shard_map/ppermute | solution.py:202
  52.6 8.4 %collective-permute-start.37 = (f32[8,8]{1,0:T(8,128)S(1)}, f32[8,8]{1,0:T(8,128)S(1)}, u32[]{:S(2)}, u32[]{:S(2)}) collective-permute-start(f32[8,8]{1,0:T(8,128)S(1)} %get-tuple-element.7), channel_id=1, source_target_pairs={{0,21},{1,22},{2,23},{3,24},{4,25},{5,26},{6,27},{7,28},{8,29},{9,... | collective-permute-start | bytes 776 | tf_op jit(solution)/shard_map/ppermute | solution.py:202
  53.9 8.8 %collective-permute-start.36 = (f32[8,8]{1,0:T(8,128)S(1)}, f32[8,8]{1,0:T(8,128)S(1)}, u32[]{:S(2)}, u32[]{:S(2)}) collective-permute-start(f32[8,8]{1,0:T(8,128)S(1)} %get-tuple-element.7), channel_id=1, source_target_pairs={{0,20},{1,21},{2,22},{3,23},{4,24},{5,25},{6,26},{7,27},{8,28},{9,... | collective-permute-start | bytes 776 | tf_op jit(solution)/shard_map/ppermute | solution.py:202
  55.5 8.9 %collective-permute-start.35 = (f32[8,8]{1,0:T(8,128)S(1)}, f32[8,8]{1,0:T(8,128)S(1)}, u32[]{:S(2)}, u32[]{:S(2)}) collective-permute-start(f32[8,8]{1,0:T(8,128)S(1)} %get-tuple-element.7), channel_id=1, source_target_pairs={{0,19},{1,20},{2,21},{3,22},{4,23},{5,24},{6,25},{7,26},{8,27},{9,... | collective-permute-start | bytes 776 | tf_op jit(solution)/shard_map/ppermute | solution.py:202
  58.4 6.6 %collective-permute-start.34 = (f32[8,8]{1,0:T(8,128)S(1)}, f32[8,8]{1,0:T(8,128)S(1)}, u32[]{:S(2)}, u32[]{:S(2)}) collective-permute-start(f32[8,8]{1,0:T(8,128)S(1)} %get-tuple-element.7), channel_id=1, source_target_pairs={{0,18},{1,19},{2,20},{3,21},{4,22},{5,23},{6,24},{7,25},{8,26},{9,... | collective-permute-start | bytes 776 | tf_op jit(solution)/shard_map/ppermute | solution.py:202
  62.6 6.7 %collective-permute-start.32 = (f32[8,8]{1,0:T(8,128)S(1)}, f32[8,8]{1,0:T(8,128)S(1)}, u32[]{:S(2)}, u32[]{:S(2)}) collective-permute-start(f32[8,8]{1,0:T(8,128)S(1)} %get-tuple-element.7), channel_id=1, source_target_pairs={{0,16},{1,17},{2,18},{3,19},{4,20},{5,21},{6,22},{7,23},{8,24},{9,... | collective-permute-start | bytes 776 | tf_op jit(solution)/shard_map/ppermute | solution.py:202
  64.5 6.8 %collective-permute-start.31 = (f32[8,8]{1,0:T(8,128)S(1)}, f32[8,8]{1,0:T(8,128)S(1)}, u32[]{:S(2)}, u32[]{:S(2)}) collective-permute-start(f32[8,8]{1,0:T(8,128)S(1)} %get-tuple-element.7), channel_id=1, source_target_pairs={{0,15},{1,16},{2,17},{3,18},{4,19},{5,20},{6,21},{7,22},{8,23},{9,... | collective-permute-start | bytes 776 | tf_op jit(solution)/shard_map/ppermute | solution.py:202
  65.0 6.3 %collective-permute-start.30 = (f32[8,8]{1,0:T(8,128)S(1)}, f32[8,8]{1,0:T(8,128)S(1)}, u32[]{:S(2)}, u32[]{:S(2)}) collective-permute-start(f32[8,8]{1,0:T(8,128)S(1)} %get-tuple-element.7), channel_id=1, source_target_pairs={{0,14},{1,15},{2,16},{3,17},{4,18},{5,19},{6,20},{7,21},{8,22},{9,... | collective-permute-start | bytes 776 | tf_op jit(solution)/shard_map/ppermute | solution.py:202
  65.9 7.3 %collective-permute-start.29 = (f32[8,8]{1,0:T(8,128)S(1)}, f32[8,8]{1,0:T(8,128)S(1)}, u32[]{:S(2)}, u32[]{:S(2)}) collective-permute-start(f32[8,8]{1,0:T(8,128)S(1)} %get-tuple-element.7), channel_id=1, source_target_pairs={{0,13},{1,14},{2,15},{3,16},{4,17},{5,18},{6,19},{7,20},{8,21},{9,... | collective-permute-start | bytes 776 | tf_op jit(solution)/shard_map/ppermute | solution.py:202
  71.2 6.3 %collective-permute-start.27 = (f32[8,8]{1,0:T(8,128)S(1)}, f32[8,8]{1,0:T(8,128)S(1)}, u32[]{:S(2)}, u32[]{:S(2)}) collective-permute-start(f32[8,8]{1,0:T(8,128)S(1)} %get-tuple-element.7), channel_id=1, source_target_pairs={{0,11},{1,12},{2,13},{3,14},{4,15},{5,16},{6,17},{7,18},{8,19},{9,... | collective-permute-start | bytes 776 | tf_op jit(solution)/shard_map/ppermute | solution.py:202
  71.3 7.1 %collective-permute-start.26 = (f32[8,8]{1,0:T(8,128)S(1)}, f32[8,8]{1,0:T(8,128)S(1)}, u32[]{:S(2)}, u32[]{:S(2)}) collective-permute-start(f32[8,8]{1,0:T(8,128)S(1)} %get-tuple-element.7), channel_id=1, source_target_pairs={{0,10},{1,11},{2,12},{3,13},{4,14},{5,15},{6,16},{7,17},{8,18},{9,... | collective-permute-start | bytes 776 | tf_op jit(solution)/shard_map/ppermute | solution.py:202
  74.7 7.5 %collective-permute-start.24 = (f32[8,8]{1,0:T(8,128)S(1)}, f32[8,8]{1,0:T(8,128)S(1)}, u32[]{:S(2)}, u32[]{:S(2)}) collective-permute-start(f32[8,8]{1,0:T(8,128)S(1)} %get-tuple-element.7), channel_id=1, source_target_pairs={{0,8},{1,9},{2,10},{3,11},{4,12},{5,13},{6,14},{7,15},{8,16},{9,17... | collective-permute-start | bytes 776 | tf_op jit(solution)/shard_map/ppermute | solution.py:202
  77.5 6.3 %collective-permute-start.23 = (f32[8,8]{1,0:T(8,128)S(1)}, f32[8,8]{1,0:T(8,128)S(1)}, u32[]{:S(2)}, u32[]{:S(2)}) collective-permute-start(f32[8,8]{1,0:T(8,128)S(1)} %get-tuple-element.7), channel_id=1, source_target_pairs={{0,7},{1,8},{2,9},{3,10},{4,11},{5,12},{6,13},{7,14},{8,15},{9,16}... | collective-permute-start | bytes 776 | tf_op jit(solution)/shard_map/ppermute | solution.py:202
  78.9 7.9 %collective-permute-start.21 = (f32[8,8]{1,0:T(8,128)S(1)}, f32[8,8]{1,0:T(8,128)S(1)}, u32[]{:S(2)}, u32[]{:S(2)}) collective-permute-start(f32[8,8]{1,0:T(8,128)S(1)} %get-tuple-element.7), channel_id=1, source_target_pairs={{0,5},{1,6},{2,7},{3,8},{4,9},{5,10},{6,11},{7,12},{8,13},{9,14},{... | collective-permute-start | bytes 776 | tf_op jit(solution)/shard_map/ppermute | solution.py:202
  82.2 6.3 %collective-permute-start.20 = (f32[8,8]{1,0:T(8,128)S(1)}, f32[8,8]{1,0:T(8,128)S(1)}, u32[]{:S(2)}, u32[]{:S(2)}) collective-permute-start(f32[8,8]{1,0:T(8,128)S(1)} %get-tuple-element.7), channel_id=1, source_target_pairs={{0,4},{1,5},{2,6},{3,7},{4,8},{5,9},{6,10},{7,11},{8,12},{9,13},{1... | collective-permute-start | bytes 776 | tf_op jit(solution)/shard_map/ppermute | solution.py:202
  83.8 7.2 %collective-permute-start.19 = (f32[8,8]{1,0:T(8,128)S(1)}, f32[8,8]{1,0:T(8,128)S(1)}, u32[]{:S(2)}, u32[]{:S(2)}) collective-permute-start(f32[8,8]{1,0:T(8,128)S(1)} %get-tuple-element.7), channel_id=1, source_target_pairs={{0,3},{1,4},{2,5},{3,6},{4,7},{5,8},{6,9},{7,10},{8,11},{9,12},{10... | collective-permute-start | bytes 776 | tf_op jit(solution)/shard_map/ppermute | solution.py:202
  83.9 7.1 %collective-permute-start.18 = (f32[8,8]{1,0:T(8,128)S(1)}, f32[8,8]{1,0:T(8,128)S(1)}, u32[]{:S(2)}, u32[]{:S(2)}) collective-permute-start(f32[8,8]{1,0:T(8,128)S(1)} %get-tuple-element.7), channel_id=1, source_target_pairs={{0,2},{1,3},{2,4},{3,5},{4,6},{5,7},{6,8},{7,9},{8,10},{9,11},{10,... | collective-permute-start | bytes 776 | tf_op jit(solution)/shard_map/ppermute | solution.py:202
  84.0 7.3 %collective-permute-start.17 = (f32[8,8]{1,0:T(8,128)S(1)}, f32[8,8]{1,0:T(8,128)S(1)}, u32[]{:S(2)}, u32[]{:S(2)}) collective-permute-start(f32[8,8]{1,0:T(8,128)S(1)} %get-tuple-element.7), channel_id=1, source_target_pairs={{0,1},{1,2},{2,3},{3,4},{4,5},{5,6},{6,7},{7,8},{8,9},{9,10},{10,1... | collective-permute-start | bytes 776 | tf_op jit(solution)/shard_map/ppermute | solution.py:202
  (20 other events, 89.7 us)

commit v3 on v2

--- a/solution.py
+++ b/solution.py
@@ -11,24 +11,21 @@
 LANES = 128
 SUB = 8
 CHUNK = 64
-WIDEST = 32
 
 NT = (((1,), (1,)), ((), ()))
 
 
 def tile_kernel(
-    n_row, n_col, side, rows_s, cols_s, count_s, ener, tiles, *refs,
+    n_col, side, rows_s, cols_s, count_s, ener, tiles, gath, *refs,
 ):
-    gath, refs = refs[:n_row], refs[n_row:]
     seg, refs = refs[:n_col], refs[n_col:]
     own_ref, send_ref, terms_ref, buf, table, picked, select, part, sems, *acc = refs
-    kvec, own = gath[0].shape
+    n_row, kvec, own = gath.shape
     slots = tiles.shape[0]
     blk_own = own // side
     per = LANES // side
     n_chunk = tiles.shape[1] // LANES
     count = count_s[0]
-    my_row = lax.axis_index("row")
     my_col = lax.axis_index("col")
 
     def tile_copy(ch):
@@ -47,12 +44,11 @@
     low = lane < side
     zero = jnp.zeros((kvec, LANES), jnp.float32)
 
-    for s in range(n_row):
-        first = lax.rem(my_row + (n_row - s), n_row) * blk_own
+    for r in range(n_row):
         for p in range(own // LANES):
-            x = gath[s][:, p * LANES:(p + 1) * LANES].astype(jnp.float32)
+            x = gath[r, :, p * LANES:(p + 1) * LANES].astype(jnp.float32)
             y = pltpu.roll(x, side, 1)
-            at = first + p * per
+            at = r * blk_own + p * per
             even = jnp.concatenate([jnp.where(low, x, zero), jnp.where(low, zero, y)], axis=0)
             odd = jnp.concatenate([jnp.where(low, y, zero), jnp.where(low, zero, x)], axis=0)
             table[at] = even.astype(jnp.bfloat16)
@@ -156,8 +152,8 @@
 
 
 def tile_work(rows, cols, count, gath, seg, ener, tiles):
-    n_row, n_col = len(gath), len(seg)
-    kvec, own = gath[0].shape
+    n_col = len(seg)
+    n_row, kvec, own = gath.shape
     slots, area = tiles.shape
     side = math.isqrt(area)
     per = LANES // side
@@ -167,14 +163,14 @@
     vmem = pl.BlockSpec(memory_space=pltpu.VMEM)
     smem = pl.BlockSpec(memory_space=pltpu.SMEM)
     return pl.pallas_call(
-        functools.partial(tile_kernel, n_row, n_col, side),
+        functools.partial(tile_kernel, n_col, side),
         out_shape=(
             jax.ShapeDtypeStruct((kvec, own), jnp.float32),
             jax.ShapeDtypeStruct((n_col - 1, kvec, own), jnp.bfloat16),
             jax.ShapeDtypeStruct((kvec, kvec), jnp.float32),
         ),
         in_specs=[smem, smem, smem, vmem, pl.BlockSpec(memory_space=pl.ANY)]
-        + [vmem] * (n_row + n_col),
+        + [vmem] * (1 + n_col),
         out_specs=(vmem, vmem, vmem),
         scratch_shapes=[
             pltpu.VMEM((slots, area), jnp.bfloat16),
@@ -189,37 +185,28 @@
             flops=2 * slots * area * kvec, bytes_accessed=2 * slots * area, transcendentals=0
         ),
         name="tile_work",
-    )(rows, cols, count, ener, tiles, *gath, *seg)
-
-
-def from_all(x, axes, size, group, stride):
+    )(rows, cols, count, ener, tiles, gath, *seg)
+
+
+def from_all(x, axis, size):
     got = [x]
-    for s in range(1, group):
-        perm = []
-        for i in range(size):
-            place = i // stride % group
-            perm.append((i, i + ((place + s) % group - place) * stride))
-        got.append(lax.ppermute(x, axes, perm))
+    for s in range(1, size):
+        got.append(lax.ppermute(x, axis, [(i, (i + s) % size) for i in range(size)]))
     return got
 
 
-def sum_everywhere(x, axes, size):
-    stride = 1
-    while stride < size:
-        group = math.gcd(size // stride, WIDEST)
-        if group == 1:
-            group = size // stride
-        x = sum(from_all(x, axes, size, group, stride))
-        stride *= group
-    return x
+def exchange(x, axes, size):
+    copies = jnp.broadcast_to(x[None], (size,) + x.shape)
+    return lax.all_to_all(copies, axes, 0, 0)
 
 
 def per_device(vectors, energies, tiles, tile_rows, tile_cols, tile_count):
     kvec, own = vectors.shape
     n_row = lax.axis_size("row")
     n_col = lax.axis_size("col")
-    seg = from_all(vectors, "col", n_col, n_col, 1)
-    gath = from_all(vectors, "row", n_row, n_row, 1)
+    devices = n_row * n_col
+    seg = from_all(vectors, "col", n_col)
+    gath = exchange(vectors, "row", n_row)
     base, send, terms = tile_work(
         tile_rows, tile_cols, tile_count, gath, seg, energies[None, :], tiles
     )
@@ -227,7 +214,7 @@
     for s in range(1, n_col):
         got = lax.ppermute(send[s - 1], "col", [(c, (c + s) % n_col) for c in range(n_col)])
         whole = whole + got.astype(jnp.float32)
-    gram = sum_everywhere(terms, ("row", "col"), n_row * n_col) / (n_row * n_col * own)
+    gram = jnp.sum(exchange(terms, ("row", "col"), devices), axis=0) / (devices * own)
     vec32 = vectors.astype(jnp.float32)
     residual = whole - jnp.einsum("ab,an->bn", gram, vec32, precision=lax.Precision.HIGHEST)
     return (whole.astype(jnp.bfloat16), residual)

time: 93.6 us -> 44 us (0.47); the launches traced: 92.2 us -> 43.7 us
  starting transfers between devices: 65.9 us -> 9.27 us
  blocking collectives: 0 us -> 14.2 us
  waiting for transfers between devices: 16.3 us -> 7.81 us
  local copies, waits for them, and re-layouts: 2.78 us -> 4.3 us
  Pallas kernels: 4.43 us -> 5.37 us
    ppermute x47 -> x1, starting transfers between devices: 65.8 us -> 1.58 us  [from_all(): lax.ppermute(x, axis, [(i, (i + s) % size) for i in range(size)])]
    ppermute x47 -> x1, waiting for transfers between devices: 16.3 us -> 1.78 us  [from_all(): lax.ppermute(x, axis, [(i, (i + s) % size) for i in range(size)])]
    all_to_all x0 -> x1, blocking collectives: none -> 14.2 us  [exchange(): return lax.all_to_all(copies, axes, 0, 0)]
    all_to_all x0 -> x1, starting transfers between devices: none -> 7.36 us  [exchange(): return lax.all_to_all(copies, axes, 0, 0)]
    all_to_all x0 -> x1, waiting for transfers between devices: none -> 6.03 us  [exchange(): return lax.all_to_all(copies, axes, 0, 0)]
    broadcast_in_dim x0 -> x2, local copies, waits for them, and re-layouts: none -> 1.51 us  [exchange(): copies = jnp.broadcast_to(x[None], (size,) + x.shape)]
    pallas_call x1, Pallas kernels: 4.43 us -> 5.37 us  [tile_work(): pl.pallas_call(functools.partial(tile_kernel, n_col, side), out_shape=(ja...]
    unnamed x8 -> x10, local copies, waits for them, and re-layouts: 2.78 us -> 2.78 us
  transfers between devices with their start and end apart: 48 -> 3, of which waited for: 11 -> 2; matrix products, arithmetic and copies ran while one was open for 1% -> 0% of each run, Pallas kernels for 0% -> 0%
where the time goes in v3:
time: 44 us; the launch traced here: 43.7 us
  blocking collectives  14.2 us (32%)
  starting transfers between devices  9.27 us (21%)
  waiting for transfers between devices  7.81 us (18%)
  Pallas kernels  5.37 us (12%)
  local copies, waits for them, and re-layouts  4.3 us (10%)
  between operations  1.32 us (3%)
  matrix products  0.82 us (2%)
  other arithmetic  0.65 us (1%)
    all_to_all x1, blocking collectives, exchange(): return lax.all_to_all(copies, axes, 0, 0)  14.2 us
    all_to_all x1, starting transfers between devices, exchange(): return lax.all_to_all(copies, axes, 0, 0)  7.36 us
    all_to_all x1, waiting for transfers between devices, exchange(): return lax.all_to_all(copies, axes, 0, 0)  6.03 us
    pallas_call x1, Pallas kernels, tile_work(): pl.pallas_call(functools.partial(tile_kernel, n_col, side), out_shape=(ja...  5.37 us
    unnamed x10, local copies, waits for them, and re-layouts  2.78 us
    ppermute x1, waiting for transfers between devices, from_all(): lax.ppermute(x, axis, [(i, (i + s) % size) for i in range(size)])  1.78 us
    ppermute x1, starting transfers between devices, from_all(): lax.ppermute(x, axis, [(i, (i + s) % size) for i in range(size)])  1.58 us
    broadcast_in_dim x2, local copies, waits for them, and re-layouts, exchange(): copies = jnp.broadcast_to(x[None], (size,) + x.shape)  1.51 us
  transfers between devices with their start and end apart: 3, of which 2 were waited for; matrix products, arithmetic and copies ran while one was open for 0% of the time, Pallas kernels for 0%

profile of v3, /device:TPU:0, one launch (start us, length us, event | category | flops | bytes accessed | tf_op | source)
XLA Modules:
  0.0 43.7 jit_solution(9240801330993794687)
XLA Ops:
  0.6 0.0 copy-start.1
  0.6 1.5 %broadcast_in_dim.7 = bf16[16,8,1024]{2,1,0:T(8,128)(2,1)} broadcast(bf16[8,1024]{1,0:T(8,128)(2,1)} %refs_0_.1), dimensions={1,2} | broadcast | bytes 278528 | tf_op jit(solution)/shard_map/broadcast_in_dim | solution.py:199
  2.1 7.4 %all-to-all-start = ((bf16[16,8,1024]{2,1,0:T(8,128)(2,1)}), bf16[16,8,1024]{2,1,0:T(8,128)(2,1)S(1)}, u32[]{:S(2)}, u32[]{:S(2)}) async-start(bf16[16,8,1024]{2,1,0:T(8,128)(2,1)} %broadcast_in_dim.7), calls=%async_computation | async-start | bytes 524288 | tf_op jit(solution)/shard_map/all_to_all | solution.py:200
  9.5 1.6 %collective-permute-start = (bf16[8,1024]{1,0:T(8,128)(2,1)}, bf16[8,1024]{1,0:T(8,128)(2,1)S(1)}, u32[]{:S(2)}, u32[]{:S(2)}) collective-permute-start(bf16[8,1024]{1,0:T(8,128)(2,1)} %refs_0_.1), channel_id=1, source_target_pairs={{0,1},{1,0},{2,3},{3,2},{4,5},{5,4},{6,7},{7,6},{8,9},{9,8},{10,11... | collective-permute-start | bytes 49160 | tf_op jit(solution)/shard_map/ppermute | solution.py:194
  11.7 1.8 %collective-permute-done.refs_1_ = bf16[8,1024]{1,0:T(8,128)(2,1)S(1)} collective-permute-done((bf16[8,1024]{1,0:T(8,128)(2,1)}, bf16[8,1024]{1,0:T(8,128)(2,1)S(1)}, u32[]{:S(2)}, u32[]{:S(2)}) %collective-permute-start) | collective-permute-done | bytes 16416 | tf_op jit(solution)/shard_map/ppermute | solution.py:194
  13.5 6.0 %all-to-all-done.gath = bf16[16,8,1024]{2,1,0:T(8,128)(2,1)S(1)} async-done(((bf16[16,8,1024]{2,1,0:T(8,128)(2,1)}), bf16[16,8,1024]{2,1,0:T(8,128)(2,1)S(1)}, u32[]{:S(2)}, u32[]{:S(2)}) %all-to-all-start) | async-done | bytes 262176 | tf_op jit(solution)/shard_map/all_to_all | solution.py:200
  19.6 0.0 copy-start
  19.6 0.7 %copy-done = bf16[8,1024]{1,0:T(8,128)(2,1)S(1)} copy-done((bf16[8,1024]{1,0:T(8,128)(2,1)S(1)}, bf16[8,1024]{1,0:T(8,128)(2,1)}, u32[]{:S(2)}) %copy-start) | copy-done | bytes 16408
  20.3 0.0 copy-start.2
  20.3 0.7 %copy-done.2 = s32[1024]{0:T(1024)S(1)} copy-done((s32[1024]{0:T(1024)S(1)}, s32[1024]{0:T(1024)}, u32[]{:S(2)}) %copy-start.2) | copy-done | bytes 4120
  21.0 0.0 copy-start.3
  21.0 0.7 %copy-done.3 = s32[1024]{0:T(1024)S(1)} copy-done((s32[1024]{0:T(1024)S(1)}, s32[1024]{0:T(1024)}, u32[]{:S(2)}) %copy-start.3) | copy-done | bytes 4120
  21.7 0.0 copy-start.4
  21.7 0.7 %copy-done.4 = f32[1024]{0:T(1024)S(1)} copy-done((f32[1024]{0:T(1024)S(1)}, f32[1024]{0:T(1024)}, u32[]{:S(2)}) %copy-start.4) | copy-done | bytes 4120
  22.3 5.4 %tile_work.1 = (f32[8,1024]{1,0:T(8,128)S(1)}, bf16[1,8,1024]{2,1,0:T(8,128)(2,1)S(1)}, f32[8,8]{1,0:T(8,128)S(1)}) custom-call(s32[1024]{0:T(1024)S(1)} %copy-done.2, s32[1024]{0:T(1024)S(1)} %copy-done.3, s32[1]{0:T(128)S(6)} %copy.10.count_s, f32[1,1024]{1,0:T(1,128)S(1)} %bitcast.3, bf16[1024,4096]{1,0:T(8,128)(2,1)} %tiles.1, ...), custom_call_target="tpu_custom_call" | custom-call | flops 67108864 | bytes 8388608 | tf_op jit(solution)/shard_map/tile_work/pallas_call | solution.py:165
  27.7 0.3 collective-permute-start.1
  28.1 14.2 %all_to_all.10 = f32[32,8,8]{2,1,0:T(8,128)S(1)} all-to-all(f32[32,8,8]{2,1,0:T(8,128)S(1)} %broadcast_in_dim.8), channel_id=1, replica_groups=mesh['row'=16,'col'=2] {'row','col'}, dimensions={0} | all-to-all | bytes 16384 | tf_op jit(solution)/shard_map/all_to_all | solution.py:200
  42.3 0.0 collective-permute-done.1
  42.3 0.6 %fusion = bf16[8,1024]{1,0:T(8,128)(2,1)} fusion(f32[8,1024]{1,0:T(8,128)S(1)} %get-tuple-element.5, bf16[8,1024]{1,0:T(8,128)(2,1)S(1)} %collective-permute-done.1), kind=kLoop, calls=%fused_computation.2 | loop fusion | flops 24576 | bytes 65536 | tf_op jit(solution)/shard_map/convert_element_type | solution.py:220
  42.9 0.0 copy-done.1
  42.9 0.8 %convolution_subtract_fusion = f32[8,1024]{1,0:T(8,128)} fusion(bf16[8,1024]{1,0:T(8,128)(2,1)S(1)} %copy-done.1, f32[8,1024]{1,0:T(8,128)S(1)} %get-tuple-element.5, bf16[8,1024]{1,0:T(8,128)(2,1)S(1)} %collective-permute-done.1, f32[8,8]{1,0:T(8,128)S(1)} %reduce_sum.9), kind=kOutput, calls=%fused_computation | convolution fusion | flops 811072 | bytes 98560 | tf_op jit(solution)/shard_map/ab,an->bn/dot_general | solution.py:219
  (2 shorter events, 0.0 us)
Async XLA Ops:
  0.6 42.2 %copy-start.1 = (bf16[8,1024]{1,0:T(8,128)(2,1)S(1)}, bf16[8,1024]{1,0:T(8,128)(2,1)}, u32[]{:S(2)}) copy-start(bf16[8,1024]{1,0:T(8,128)(2,1)} %refs_0_.1) | copy-start | bytes 49156
  2.1 17.4 %all-to-all-start = ((bf16[16,8,1024]{2,1,0:T(8,128)(2,1)}), bf16[16,8,1024]{2,1,0:T(8,128)(2,1)S(1)}, u32[]{:S(2)}, u32[]{:S(2)}) async-start(bf16[16,8,1024]{2,1,0:T(8,128)(2,1)} %broadcast_in_dim.7), calls=%async_computation | async-start | bytes 524288 | tf_op jit(solution)/shard_map/all_to_all | solution.py:200
  9.5 4.0 %collective-permute-start = (bf16[8,1024]{1,0:T(8,128)(2,1)}, bf16[8,1024]{1,0:T(8,128)(2,1)S(1)}, u32[]{:S(2)}, u32[]{:S(2)}) collective-permute-start(bf16[8,1024]{1,0:T(8,128)(2,1)} %refs_0_.1), channel_id=1, source_target_pairs={{0,1},{1,0},{2,3},{3,2},{4,5},{5,4},{6,7},{7,6},{8,9},{9,8},{10,11... | collective-permute-start | bytes 49160 | tf_op jit(solution)/shard_map/ppermute | solution.py:194
  19.6 0.7 %copy-start = (bf16[8,1024]{1,0:T(8,128)(2,1)S(1)}, bf16[8,1024]{1,0:T(8,128)(2,1)}, u32[]{:S(2)}) copy-start(bf16[8,1024]{1,0:T(8,128)(2,1)} %refs_0_.1) | copy-start | bytes 49156
  20.3 0.7 %copy-start.2 = (s32[1024]{0:T(1024)S(1)}, s32[1024]{0:T(1024)}, u32[]{:S(2)}) copy-start(s32[1024]{0:T(1024)} %rows_s.1) | copy-start | bytes 12292
  21.0 0.7 %copy-start.3 = (s32[1024]{0:T(1024)S(1)}, s32[1024]{0:T(1024)}, u32[]{:S(2)}) copy-start(s32[1024]{0:T(1024)} %cols_s.1) | copy-start | bytes 12292
  21.7 0.7 %copy-start.4 = (f32[1024]{0:T(1024)S(1)}, f32[1024]{0:T(1024)}, u32[]{:S(2)}) copy-start(f32[1024]{0:T(1024)} %param.7) | copy-start | bytes 12292
  27.7 14.5 %collective-permute-start.1 = (bf16[8,1024]{1,0:T(8,128)(2,1)S(1)}, bf16[8,1024]{1,0:T(8,128)(2,1)S(1)}, u32[]{:S(2)}, u32[]{:S(2)}) collective-permute-start(bf16[8,1024]{1,0:T(8,128)(2,1)S(1)} %bitcast.4), channel_id=1, source_target_pairs={{0,1},{1,0},{2,3},{3,2},{4,5},{5,4},{6,7},{7,6},{8,9},{9,8},{10,11... | collective-permute-start | bytes 49160 | tf_op jit(solution)/shard_map/ppermute | solution.py:215

commit v4 on v3

--- a/solution.py
+++ b/solution.py
@@ -16,22 +16,32 @@
 
 
 def tile_kernel(
-    n_col, side, rows_s, cols_s, count_s, ener, tiles, gath, *refs,
+    n_col, side, count_s, rows_h, cols_h, ener_h, tiles, gath, *refs,
 ):
     seg, refs = refs[:n_col], refs[n_col:]
-    own_ref, send_ref, terms_ref, buf, table, picked, select, part, sems, *acc = refs
+    (own_ref, send_ref, terms_ref, rows_s, cols_s, ener,
+     buf, table, picked, select, part, wide, sems, small, *acc) = refs
     n_row, kvec, own = gath.shape
     slots = tiles.shape[0]
     blk_own = own // side
     per = LANES // side
     n_chunk = tiles.shape[1] // LANES
-    count = count_s[0]
     my_col = lax.axis_index("col")
+
+    copies = [
+        pltpu.make_async_copy(src, dst, small.at[i])
+        for i, (src, dst) in enumerate(
+            ((cols_h, cols_s), (rows_h, rows_s), (ener_h, ener))
+        )
+    ]
+    for copy in copies:
+        copy.start()
 
     def tile_copy(ch):
         span = pl.ds(pl.multiple_of(ch * CHUNK, CHUNK), CHUNK)
         return pltpu.make_async_copy(tiles.at[span], buf.at[span], sems.at[ch])
 
+    count = count_s[0]
     used = (count + CHUNK - 1) // CHUNK
 
     def start(ch, carry):
@@ -56,9 +66,10 @@
     n_blocks = n_row * blk_own
     table[n_blocks] = jnp.zeros((per * kvec, LANES), jnp.bfloat16)
 
+    for copy in copies:
+        copy.wait()
     n_seg = acc[0].shape[0]
     width = n_chunk * SUB
-    depth = per * per * width
 
     def clear(r, carry):
         for a in acc:
@@ -145,10 +156,15 @@
         if s > 0:
             send_ref[s - 1] = share.astype(jnp.bfloat16)
         terms = terms + lax.dot_general(
-            seg[(n_col - s) % n_col][...].astype(jnp.float32), share, NT,
+            share, seg[(n_col - s) % n_col][...].astype(jnp.float32), NT,
             precision=lax.Precision.HIGHEST, preferred_element_type=jnp.float32,
         )
-    terms_ref[...] = terms
+    wide[...] = jnp.zeros(wide.shape, jnp.float32)
+    wide[:, :kvec] = terms
+    spaced = pltpu.roll(wide[...], 0, 1, stride=kvec, stride_axis=0)
+    flat = jnp.sum(spaced, axis=0, keepdims=True)
+    for i in range(terms_ref.shape[0]):
+        terms_ref[i] = flat
 
 
 def tile_work(rows, cols, count, gath, seg, ener, tiles):
@@ -161,63 +177,113 @@
     n_seg = n_col * blk_own
     width = area // LANES * SUB
     vmem = pl.BlockSpec(memory_space=pltpu.VMEM)
-    smem = pl.BlockSpec(memory_space=pltpu.SMEM)
+    far_away = pl.BlockSpec(memory_space=pltpu.HBM)
     return pl.pallas_call(
         functools.partial(tile_kernel, n_col, side),
         out_shape=(
             jax.ShapeDtypeStruct((kvec, own), jnp.float32),
             jax.ShapeDtypeStruct((n_col - 1, kvec, own), jnp.bfloat16),
-            jax.ShapeDtypeStruct((kvec, kvec), jnp.float32),
+            jax.ShapeDtypeStruct((n_row * n_col, 1, LANES), jnp.float32),
         ),
-        in_specs=[smem, smem, smem, vmem, pl.BlockSpec(memory_space=pl.ANY)]
-        + [vmem] * (1 + n_col),
+        in_specs=[pl.BlockSpec(memory_space=pltpu.SMEM)] + [far_away] * 4 + [vmem] * (1 + n_col),
         out_specs=(vmem, vmem, vmem),
         scratch_shapes=[
+            pltpu.SMEM((slots,), jnp.int32),
+            pltpu.SMEM((slots,), jnp.int32),
+            pltpu.VMEM((1, own), jnp.float32),
             pltpu.VMEM((slots, area), jnp.bfloat16),
             pltpu.VMEM((n_row * blk_own + 1, per * kvec, LANES), jnp.bfloat16),
             pltpu.VMEM((n_seg // per * 2 * kvec, per * per * width), jnp.bfloat16),
             pltpu.VMEM((per * per * width, LANES), jnp.bfloat16),
             pltpu.VMEM((n_col, kvec, own), jnp.float32),
+            pltpu.VMEM((kvec, LANES), jnp.float32),
             pltpu.SemaphoreType.DMA((slots // CHUNK,)),
+            pltpu.SemaphoreType.DMA((3,)),
         ] + [pltpu.VMEM((n_seg, per * kvec, width), jnp.float32)] * SUB,
         compiler_params=pltpu.CompilerParams(vmem_limit_bytes=48 * 2**20),
         cost_estimate=pl.CostEstimate(
             flops=2 * slots * area * kvec, bytes_accessed=2 * slots * area, transcendentals=0
         ),
         name="tile_work",
-    )(rows, cols, count, ener, tiles, gath, *seg)
-
-
-def from_all(x, axis, size):
+    )(count, *[pltpu.with_memory_space_constraint(x, pltpu.HBM) for x in (rows, cols, ener, tiles)],
+      gath, *seg)
+
+
+def finish_kernel(scale, base, gram_parts, vec, *refs):
+    got, (product, residual) = refs[:-2], refs[-2:]
+    whole = base[...]
+    for piece in got:
+        whole = whole + piece[...].astype(jnp.float32)
+    product[...] = whole.astype(jnp.bfloat16)
+    flat = gram_parts[0]
+    for i in range(1, gram_parts.shape[0]):
+        flat = flat + gram_parts[i]
+    kvec = vec.shape[0]
+    lane = lax.broadcasted_iota(jnp.int32, (kvec, LANES), 1)
+    first = kvec * lax.broadcasted_iota(jnp.int32, (kvec, LANES), 0)
+    wide = jnp.broadcast_to(flat * scale, (kvec, LANES))
+    vec32 = vec[...].astype(jnp.float32)
+    for a in range(kvec):
+        column = jnp.sum(jnp.where(lane == first + a, wide, 0.0), axis=1, keepdims=True)
+        whole = whole - column * vec32[a:a + 1, :]
+    residual[...] = whole
+
+
+def finish(scale, base, gram_parts, vectors, got):
+    vmem = pl.BlockSpec(memory_space=pltpu.VMEM)
+    return pl.pallas_call(
+        functools.partial(finish_kernel, scale),
+        out_shape=(
+            jax.ShapeDtypeStruct(vectors.shape, jnp.bfloat16),
+            jax.ShapeDtypeStruct(vectors.shape, jnp.float32),
+        ),
+        in_specs=[vmem] * (3 + len(got)),
+        out_specs=(vmem, vmem),
+        compiler_params=pltpu.CompilerParams(vmem_limit_bytes=4 * 2**20),
+        name="finish",
+    )(base, gram_parts, vectors, *got)
+
+
+def from_all(x, axis):
+    size = lax.axis_size(axis)
     got = [x]
     for s in range(1, size):
         got.append(lax.ppermute(x, axis, [(i, (i + s) % size) for i in range(size)]))
     return got
 
 
-def exchange(x, axes, size):
-    copies = jnp.broadcast_to(x[None], (size,) + x.shape)
-    return lax.all_to_all(copies, axes, 0, 0)
+def copies_kernel(x, out):
+    for i in range(out.shape[0]):
+        out[i] = x[...]
+
+
+def repeat(x, size):
+    vmem = pl.BlockSpec(memory_space=pltpu.VMEM)
+    return pl.pallas_call(
+        copies_kernel,
+        out_shape=jax.ShapeDtypeStruct((size,) + x.shape, x.dtype),
+        in_specs=[vmem],
+        out_specs=vmem,
+        compiler_params=pltpu.CompilerParams(vmem_limit_bytes=4 * 2**20),
+        name="copies",
+    )(x)
 
 
 def per_device(vectors, energies, tiles, tile_rows, tile_cols, tile_count):
     kvec, own = vectors.shape
     n_row = lax.axis_size("row")
     n_col = lax.axis_size("col")
-    devices = n_row * n_col
-    seg = from_all(vectors, "col", n_col)
-    gath = exchange(vectors, "row", n_row)
+    gath = lax.all_to_all(repeat(vectors, n_row), "row", 0, 0)
+    seg = from_all(vectors, "col")
     base, send, terms = tile_work(
         tile_rows, tile_cols, tile_count, gath, seg, energies[None, :], tiles
     )
-    whole = base
-    for s in range(1, n_col):
-        got = lax.ppermute(send[s - 1], "col", [(c, (c + s) % n_col) for c in range(n_col)])
-        whole = whole + got.astype(jnp.float32)
-    gram = jnp.sum(exchange(terms, ("row", "col"), devices), axis=0) / (devices * own)
-    vec32 = vectors.astype(jnp.float32)
-    residual = whole - jnp.einsum("ab,an->bn", gram, vec32, precision=lax.Precision.HIGHEST)
-    return (whole.astype(jnp.bfloat16), residual)
+    got = [
+        lax.ppermute(send[s - 1], "col", [(c, (c + s) % n_col) for c in range(n_col)])
+        for s in range(1, n_col)
+    ]
+    gram_parts = lax.all_to_all(terms, ("row", "col"), 0, 0)
+    return finish(1.0 / (n_row * n_col * own), base, gram_parts, vectors, got)
 
 
 def solution(mesh):

time: 44 us -> 38.9 us (0.88)
  blocking collectives: 14.2 us -> 0 us
  starting transfers between devices: 9.27 us -> 16 us
  waiting for transfers between devices: 7.81 us -> 13.1 us
  local copies, waits for them, and re-layouts: 4.3 us -> 1.43 us
  Pallas kernels: 5.37 us -> 6.38 us
  matrix products: 0.82 us -> 0 us
  other arithmetic: 0.65 us -> 0 us
    all_to_all x1 -> x0, blocking collectives: 14.2 us -> none  [exchange(): return lax.all_to_all(copies, axes, 0, 0)]
    all_to_all x1 -> x2, starting transfers between devices: 7.36 us -> 12.6 us  [the longest x1 7.36 us: per_device(): gath = lax.all_to_all(repeat(vectors, n_row), 'row', 0, 0)]
    all_to_all x1 -> x2, waiting for transfers between devices: 6.03 us -> 9.33 us  [the longest x1 6.03 us: per_device(): gath = lax.all_to_all(repeat(vectors, n_row), 'row', 0, 0)]
    ppermute x1, waiting for transfers between devices: 0.01 us -> 1.99 us  [per_device(): lax.ppermute(send[s - 1], 'col', [(c, (c + s) % n_col) for c in range(n_c...]
    broadcast_in_dim x2 -> x0, local copies, waits for them, and re-layouts: 1.51 us -> none  [exchange(): copies = jnp.broadcast_to(x[None], (size,) + x.shape)]
    ppermute x1, starting transfers between devices: 0.33 us -> 1.83 us  [per_device(): lax.ppermute(send[s - 1], 'col', [(c, (c + s) % n_col) for c in range(n_c...]
    pallas_call x0 -> x2, Pallas kernels: none -> 1.47 us  [the longest x1 0.75 us: finish(): pl.pallas_call(functools.partial(finish_kernel, scale), out_shape=(jax.Sh...]
    unnamed x10 -> x6, local copies, waits for them, and re-layouts: 2.78 us -> 1.43 us
  transfers between devices with their start and end apart: 3 -> 4, of which waited for: 2 -> 4; matrix products, arithmetic and copies ran while one was open for 0% -> 0% of each run, Pallas kernels for 0% -> 0%
where the time goes in v4:
time: 38.9 us; the launch traced here: 38.2 us
  starting transfers between devices  16 us (41%)
  waiting for transfers between devices  13.1 us (34%)
  Pallas kernels  6.38 us (16%)
  local copies, waits for them, and re-layouts  1.43 us (4%)
  between operations  1.32 us (3%)
    all_to_all x1, starting transfers between devices, per_device(): gath = lax.all_to_all(repeat(vectors, n_row), 'row', 0, 0)  7.36 us
    all_to_all x1, waiting for transfers between devices, per_device(): gath = lax.all_to_all(repeat(vectors, n_row), 'row', 0, 0)  6.03 us
    all_to_all x1, starting transfers between devices, per_device(): gram_parts = lax.all_to_all(terms, ('row', 'col'), 0, 0)  5.2 us
    pallas_call x1, Pallas kernels, tile_work(): pl.pallas_call(functools.partial(tile_kernel, n_col, side), out_shape=(ja...  4.91 us
    all_to_all x1, waiting for transfers between devices, per_device(): gram_parts = lax.all_to_all(terms, ('row', 'col'), 0, 0)  3.3 us
    ppermute x1, waiting for transfers between devices, per_device(): lax.ppermute(send[s - 1], 'col', [(c, (c + s) % n_col) for c in range(n_c...  1.99 us
    ppermute x1, starting transfers between devices, per_device(): lax.ppermute(send[s - 1], 'col', [(c, (c + s) % n_col) for c in range(n_c...  1.83 us
    ppermute x1, waiting for transfers between devices, from_all(): lax.ppermute(x, axis, [(i, (i + s) % size) for i in range(size)])  1.78 us
  transfers between devices with their start and end apart: 4, of which 4 were waited for; matrix products, arithmetic and copies ran while one was open for 0% of the time, Pallas kernels for 0%

profile of v4, /device:TPU:0, one launch (start us, length us, event | category | flops | bytes accessed | tf_op | source)
XLA Modules:
  0.0 38.2 jit_solution(8404720437103357932)
XLA Ops:
  0.6 0.0 copy-start
  0.6 0.7 %copy-done = bf16[8,1024]{1,0:T(8,128)(2,1)S(1)} copy-done((bf16[8,1024]{1,0:T(8,128)(2,1)S(1)}, bf16[8,1024]{1,0:T(8,128)(2,1)}, u32[]{:S(2)}) %copy-start) | copy-done | bytes 16408
  1.3 0.0 copy-start.2
  1.4 0.7 %copies.1 = bf16[16,8,1024]{2,1,0:T(8,128)(2,1)} custom-call(bf16[8,1024]{1,0:T(8,128)(2,1)S(1)} %copy-done), custom_call_target="tpu_custom_call" | custom-call | tf_op jit(solution)/shard_map/copies/pallas_call | solution.py:262
  2.1 7.4 %all-to-all-start = ((bf16[16,8,1024]{2,1,0:T(8,128)(2,1)}), bf16[16,8,1024]{2,1,0:T(8,128)(2,1)S(1)}, u32[]{:S(2)}, u32[]{:S(2)}) async-start(bf16[16,8,1024]{2,1,0:T(8,128)(2,1)} %copies.1), calls=%async_computation | async-start | bytes 524288 | tf_op jit(solution)/shard_map/all_to_all | solution.py:276
  9.4 1.6 %collective-permute-start = (bf16[8,1024]{1,0:T(8,128)(2,1)}, bf16[8,1024]{1,0:T(8,128)(2,1)S(1)}, u32[]{:S(2)}, u32[]{:S(2)}) collective-permute-start(bf16[8,1024]{1,0:T(8,128)(2,1)} %vec.1), channel_id=1, source_target_pairs={{0,1},{1,0},{2,3},{3,2},{4,5},{5,4},{6,7},{7,6},{8,9},{9,8},{10,11... | collective-permute-start | bytes 49160 | tf_op jit(solution)/shard_map/ppermute | solution.py:251
  11.7 1.8 %collective-permute-done.refs_1_ = bf16[8,1024]{1,0:T(8,128)(2,1)S(1)} collective-permute-done((bf16[8,1024]{1,0:T(8,128)(2,1)}, bf16[8,1024]{1,0:T(8,128)(2,1)S(1)}, u32[]{:S(2)}, u32[]{:S(2)}) %collective-permute-start) | collective-permute-done | bytes 16416 | tf_op jit(solution)/shard_map/ppermute | solution.py:251
  13.4 6.0 %all-to-all-done.gath = bf16[16,8,1024]{2,1,0:T(8,128)(2,1)S(1)} async-done(((bf16[16,8,1024]{2,1,0:T(8,128)(2,1)}), bf16[16,8,1024]{2,1,0:T(8,128)(2,1)S(1)}, u32[]{:S(2)}, u32[]{:S(2)}) %all-to-all-start) | async-done | bytes 262176 | tf_op jit(solution)/shard_map/all_to_all | solution.py:276
  19.5 0.0 copy-start.1
  19.5 0.7 %copy-done.1 = bf16[8,1024]{1,0:T(8,128)(2,1)S(1)} copy-done((bf16[8,1024]{1,0:T(8,128)(2,1)S(1)}, bf16[8,1024]{1,0:T(8,128)(2,1)}, u32[]{:S(2)}) %copy-start.1) | copy-done | bytes 16408
  20.2 4.9 %tile_work.1 = (f32[8,1024]{1,0:T(8,128)S(1)}, bf16[1,8,1024]{2,1,0:T(8,128)(2,1)S(1)}, f32[32,1,128]{2,1,0:T(1,128)}) custom-call(s32[1]{0:T(128)S(6)} %copy.8.count_s, s32[1024]{0:T(1024)} %rows_h.1, s32[1024]{0:T(1024)} %cols_h.1, f32[1,1024]{1,0:T(1,128)} %bitcast.3, bf16[1024,4096]{1,0:T(8,128)(2,1)} %tiles.1, ...), custom_call_target="tpu_custom_call" | custom-call | flops 67108864 | bytes 8388608 | tf_op jit(solution)/shard_map/tile_work/pallas_call | solution.py:181
  25.1 5.2 %all-to-all-start.1 = ((f32[32,1,128]{2,1,0:T(1,128)}), f32[32,1,128]{2,1,0:T(1,128)S(1)}, u32[]{:S(2)}, u32[]{:S(2)}) async-start(f32[32,1,128]{2,1,0:T(1,128)} %get-tuple-element.6), calls=%async_computation.1 | async-start | bytes 32768 | tf_op jit(solution)/shard_map/all_to_all | solution.py:285
  30.3 1.8 %collective-permute-start.1 = (bf16[8,1024]{1,0:T(8,128)(2,1)S(1)}, bf16[8,1024]{1,0:T(8,128)(2,1)S(1)}, u32[]{:S(2)}, u32[]{:S(2)}) collective-permute-start(bf16[8,1024]{1,0:T(8,128)(2,1)S(1)} %bitcast.2), channel_id=1, source_target_pairs={{0,1},{1,0},{2,3},{3,2},{4,5},{5,4},{6,7},{7,6},{8,9},{9,8},{10,11... | collective-permute-start | bytes 49160 | tf_op jit(solution)/shard_map/ppermute | solution.py:282
  32.2 2.0 %collective-permute-done.1.refs_0_ = bf16[8,1024]{1,0:T(8,128)(2,1)S(1)} collective-permute-done((bf16[8,1024]{1,0:T(8,128)(2,1)S(1)}, bf16[8,1024]{1,0:T(8,128)(2,1)S(1)}, u32[]{:S(2)}, u32[]{:S(2)}) %collective-permute-start.1) | collective-permute-done | bytes 16416 | tf_op jit(solution)/shard_map/ppermute | solution.py:282
  34.2 3.3 %all-to-all-done.1.gram_parts = f32[32,1,128]{2,1,0:T(1,128)S(1)} async-done(((f32[32,1,128]{2,1,0:T(1,128)}), f32[32,1,128]{2,1,0:T(1,128)S(1)}, u32[]{:S(2)}, u32[]{:S(2)}) %all-to-all-start.1) | async-done | bytes 16416 | tf_op jit(solution)/shard_map/all_to_all | solution.py:285
  37.5 0.0 copy-done.2
  37.5 0.8 %finish.1 = (bf16[8,1024]{1,0:T(8,128)(2,1)}, f32[8,1024]{1,0:T(8,128)}) custom-call(f32[8,1024]{1,0:T(8,128)S(1)} %get-tuple-element.5.base, f32[32,1,128]{2,1,0:T(1,128)S(1)} %all-to-all-done.1.gram_parts, bf16[8,1024]{1,0:T(8,128)(2,1)S(1)} %copy-done.2, bf16[8,1024]{1,0:T(8,128)(2,1)S(1)} %collective-permute-done.1.refs_0_), custom_call_target="tpu_custom_call" | custom-call | tf_op jit(solution)/shard_map/finish/pallas_call | solution.py:234
Async XLA Ops:
  0.6 0.7 %copy-start = (bf16[8,1024]{1,0:T(8,128)(2,1)S(1)}, bf16[8,1024]{1,0:T(8,128)(2,1)}, u32[]{:S(2)}) copy-start(bf16[8,1024]{1,0:T(8,128)(2,1)} %vec.1) | copy-start | bytes 49156
  1.3 36.1 %copy-start.2 = (bf16[8,1024]{1,0:T(8,128)(2,1)S(1)}, bf16[8,1024]{1,0:T(8,128)(2,1)}, u32[]{:S(2)}) copy-start(bf16[8,1024]{1,0:T(8,128)(2,1)} %vec.1) | copy-start | bytes 49156
  2.1 17.4 %all-to-all-start = ((bf16[16,8,1024]{2,1,0:T(8,128)(2,1)}), bf16[16,8,1024]{2,1,0:T(8,128)(2,1)S(1)}, u32[]{:S(2)}, u32[]{:S(2)}) async-start(bf16[16,8,1024]{2,1,0:T(8,128)(2,1)} %copies.1), calls=%async_computation | async-start | bytes 524288 | tf_op jit(solution)/shard_map/all_to_all | solution.py:276
  9.4 4.0 %collective-permute-start = (bf16[8,1024]{1,0:T(8,128)(2,1)}, bf16[8,1024]{1,0:T(8,128)(2,1)S(1)}, u32[]{:S(2)}, u32[]{:S(2)}) collective-permute-start(bf16[8,1024]{1,0:T(8,128)(2,1)} %vec.1), channel_id=1, source_target_pairs={{0,1},{1,0},{2,3},{3,2},{4,5},{5,4},{6,7},{7,6},{8,9},{9,8},{10,11... | collective-permute-start | bytes 49160 | tf_op jit(solution)/shard_map/ppermute | solution.py:251
  19.5 0.7 %copy-start.1 = (bf16[8,1024]{1,0:T(8,128)(2,1)S(1)}, bf16[8,1024]{1,0:T(8,128)(2,1)}, u32[]{:S(2)}) copy-start(bf16[8,1024]{1,0:T(8,128)(2,1)} %vec.1) | copy-start | bytes 49156
  25.1 12.3 %all-to-all-start.1 = ((f32[32,1,128]{2,1,0:T(1,128)}), f32[32,1,128]{2,1,0:T(1,128)S(1)}, u32[]{:S(2)}, u32[]{:S(2)}) async-start(f32[32,1,128]{2,1,0:T(1,128)} %get-tuple-element.6), calls=%async_computation.1 | async-start | bytes 32768 | tf_op jit(solution)/shard_map/all_to_all | solution.py:285
  30.3 3.8 %collective-permute-start.1 = (bf16[8,1024]{1,0:T(8,128)(2,1)S(1)}, bf16[8,1024]{1,0:T(8,128)(2,1)S(1)}, u32[]{:S(2)}, u32[]{:S(2)}) collective-permute-start(bf16[8,1024]{1,0:T(8,128)(2,1)S(1)} %bitcast.2), channel_id=1, source_target_pairs={{0,1},{1,0},{2,3},{3,2},{4,5},{5,4},{6,7},{7,6},{8,9},{9,8},{10,11... | collective-permute-start | bytes 49160 | tf_op jit(solution)/shard_map/ppermute | solution.py:282

commit v5 on v4

--- a/solution.py
+++ b/solution.py
@@ -16,12 +16,14 @@
 
 
 def tile_kernel(
-    n_col, side, count_s, rows_h, cols_h, ener_h, tiles, gath, *refs,
+    places, relative, n_col, side, count_s, rows_h, cols_h, ener_h, tiles, *refs,
 ):
+    gath, refs = refs[:len(places)], refs[len(places):]
     seg, refs = refs[:n_col], refs[n_col:]
     (own_ref, send_ref, terms_ref, rows_s, cols_s, ener,
      buf, table, picked, select, part, wide, sems, small, *acc) = refs
-    n_row, kvec, own = gath.shape
+    kvec, own = seg[0].shape
+    n_row = sum(len(held) for held in places)
     slots = tiles.shape[0]
     blk_own = own // side
     per = LANES // side
@@ -54,15 +56,18 @@
     low = lane < side
     zero = jnp.zeros((kvec, LANES), jnp.float32)
 
-    for r in range(n_row):
-        for p in range(own // LANES):
-            x = gath[r, :, p * LANES:(p + 1) * LANES].astype(jnp.float32)
-            y = pltpu.roll(x, side, 1)
-            at = r * blk_own + p * per
-            even = jnp.concatenate([jnp.where(low, x, zero), jnp.where(low, zero, y)], axis=0)
-            odd = jnp.concatenate([jnp.where(low, y, zero), jnp.where(low, zero, x)], axis=0)
-            table[at] = even.astype(jnp.bfloat16)
-            table[at + 1] = odd.astype(jnp.bfloat16)
+    my_row = lax.axis_index("row") if relative else 0
+    for piece, held in zip(gath, places):
+        for i, place in enumerate(held):
+            first = (my_row ^ place) * blk_own
+            for p in range(own // LANES):
+                x = piece[i, :, p * LANES:(p + 1) * LANES].astype(jnp.float32)
+                y = pltpu.roll(x, side, 1)
+                at = first + p * per
+                even = jnp.concatenate([jnp.where(low, x, zero), jnp.where(low, zero, y)], axis=0)
+                odd = jnp.concatenate([jnp.where(low, y, zero), jnp.where(low, zero, x)], axis=0)
+                table[at] = even.astype(jnp.bfloat16)
+                table[at + 1] = odd.astype(jnp.bfloat16)
     n_blocks = n_row * blk_own
     table[n_blocks] = jnp.zeros((per * kvec, LANES), jnp.bfloat16)
 
@@ -167,9 +172,10 @@
         terms_ref[i] = flat
 
 
-def tile_work(rows, cols, count, gath, seg, ener, tiles):
+def tile_work(rows, cols, count, gath, places, relative, seg, ener, tiles):
     n_col = len(seg)
-    n_row, kvec, own = gath.shape
+    kvec, own = seg[0].shape
+    n_row = sum(len(held) for held in places)
     slots, area = tiles.shape
     side = math.isqrt(area)
     per = LANES // side
@@ -179,13 +185,13 @@
     vmem = pl.BlockSpec(memory_space=pltpu.VMEM)
     far_away = pl.BlockSpec(memory_space=pltpu.HBM)
     return pl.pallas_call(
-        functools.partial(tile_kernel, n_col, side),
+        functools.partial(tile_kernel, places, relative, n_col, side),
         out_shape=(
             jax.ShapeDtypeStruct((kvec, own), jnp.float32),
             jax.ShapeDtypeStruct((n_col - 1, kvec, own), jnp.bfloat16),
             jax.ShapeDtypeStruct((n_row * n_col, 1, LANES), jnp.float32),
         ),
-        in_specs=[pl.BlockSpec(memory_space=pltpu.SMEM)] + [far_away] * 4 + [vmem] * (1 + n_col),
+        in_specs=[pl.BlockSpec(memory_space=pltpu.SMEM)] + [far_away] * 4 + [vmem] * (len(gath) + n_col),
         out_specs=(vmem, vmem, vmem),
         scratch_shapes=[
             pltpu.SMEM((slots,), jnp.int32),
@@ -206,7 +212,7 @@
         ),
         name="tile_work",
     )(count, *[pltpu.with_memory_space_constraint(x, pltpu.HBM) for x in (rows, cols, ener, tiles)],
-      gath, *seg)
+      *gath, *seg)
 
 
 def finish_kernel(scale, base, gram_parts, vec, *refs):
@@ -252,6 +258,21 @@
     return got
 
 
+def gather(x, axis):
+    size = lax.axis_size(axis)
+    if size & (size - 1):
+        return [lax.all_to_all(repeat(x, size), axis, 0, 0)], [list(range(size))], False
+    pieces, places = [x[None]], [[0]]
+    step = size // 2
+    while step:
+        held = pieces[0] if len(pieces) == 1 else jnp.concatenate(pieces, axis=0)
+        got = lax.ppermute(held, axis, [(i, i ^ step) for i in range(size)])
+        places.append([step ^ place for known in places for place in known])
+        pieces.append(got)
+        step //= 2
+    return pieces, places, True
+
+
 def copies_kernel(x, out):
     for i in range(out.shape[0]):
         out[i] = x[...]
@@ -273,10 +294,10 @@
     kvec, own = vectors.shape
     n_row = lax.axis_size("row")
     n_col = lax.axis_size("col")
-    gath = lax.all_to_all(repeat(vectors, n_row), "row", 0, 0)
+    gath, places, relative = gather(vectors, "row")
     seg = from_all(vectors, "col")
     base, send, terms = tile_work(
-        tile_rows, tile_cols, tile_count, gath, seg, energies[None, :], tiles
+        tile_rows, tile_cols, tile_count, gath, places, relative, seg, energies[None, :], tiles
     )
     got = [
         lax.ppermute(send[s - 1], "col", [(c, (c + s) % n_col) for c in range(n_col)])

time: 38.9 us -> 43.8 us (1.13)
  starting transfers between devices: 16 us -> 21.1 us
  other arithmetic: 0 us -> 2.18 us
  Pallas kernels: 6.38 us -> 4.7 us
  local copies, waits for them, and re-layouts: 1.43 us -> 0.72 us
    ppermute x0 -> x4, starting transfers between devices: none -> 7.95 us  [gather(): got = lax.ppermute(held, axis, [(i, i ^ step) for i in range(size)])]
    all_to_all x1 -> x0, starting transfers between devices: 7.36 us -> none  [per_device(): gath = lax.all_to_all(repeat(vectors, n_row), 'row', 0, 0)]
    ppermute x0 -> x4, waiting for transfers between devices: none -> 6.34 us  [gather(): got = lax.ppermute(held, axis, [(i, i ^ step) for i in range(size)])]
    all_to_all x1 -> x0, waiting for transfers between devices: 6.03 us -> none  [per_device(): gath = lax.all_to_all(repeat(vectors, n_row), 'row', 0, 0)]
    all_to_all x1, starting transfers between devices: 5.2 us -> 9.38 us  [per_device(): gram_parts = lax.all_to_all(terms, ('row', 'col'), 0, 0)]
    concatenate x0 -> x3, other arithmetic: none -> 2.18 us  [gather(): held = pieces[0] if len(pieces) == 1 else jnp.concatenate(pieces, axis=0)]
    pallas_call x2 -> x1, Pallas kernels: 5.63 us -> 3.95 us  [tile_work(): pl.pallas_call(functools.partial(tile_kernel, places, relative, n_col, si...]
    unnamed x6 -> x4, local copies, waits for them, and re-layouts: 1.43 us -> 0.72 us
  transfers between devices with their start and end apart: 4 -> 7, of which waited for: 4 -> 6; matrix products, arithmetic and copies ran while one was open for 0% -> 0% of each run, Pallas kernels for 0% -> 0%
where the time goes in v5:
time: 43.8 us; the launch traced here: 43.1 us
  starting transfers between devices  21.1 us (48%)
  waiting for transfers between devices  13 us (30%)
  Pallas kernels  4.7 us (11%)
  other arithmetic  2.18 us (5%)
  between operations  1.32 us (3%)
  local copies, waits for them, and re-layouts  0.72 us (2%)
    all_to_all x1, starting transfers between devices, per_device(): gram_parts = lax.all_to_all(terms, ('row', 'col'), 0, 0)  9.38 us
    ppermute x4, starting transfers between devices, gather(): got = lax.ppermute(held, axis, [(i, i ^ step) for i in range(size)])  7.95 us
    ppermute x4, waiting for transfers between devices, gather(): got = lax.ppermute(held, axis, [(i, i ^ step) for i in range(size)])  6.34 us
    pallas_call x1, Pallas kernels, tile_work(): pl.pallas_call(functools.partial(tile_kernel, places, relative, n_col, si...  3.95 us
    all_to_all x1, waiting for transfers between devices, per_device(): gram_parts = lax.all_to_all(terms, ('row', 'col'), 0, 0)  3.3 us
    concatenate x3, other arithmetic, gather(): held = pieces[0] if len(pieces) == 1 else jnp.concatenate(pieces, axis=0)  2.18 us
    ppermute x1, waiting for transfers between devices, per_device(): lax.ppermute(send[s - 1], 'col', [(c, (c + s) % n_col) for c in range(n_c...  1.99 us
    ppermute x1, starting transfers between devices, from_all(): lax.ppermute(x, axis, [(i, (i + s) % size) for i in range(size)])  1.97 us
  transfers between devices with their start and end apart: 7, of which 6 were waited for; matrix products, arithmetic and copies ran while one was open for 0% of the time, Pallas kernels for 0%

profile of v5, /device:TPU:0, one launch (start us, length us, event | category | flops | bytes accessed | tf_op | source)
XLA Modules:
  0.0 43.1 jit_solution(9565926169619899359)
XLA Ops:
  0.6 0.0 copy-start.1
  0.6 4.1 %collective-permute-start = (bf16[1,8,1024]{2,1,0:T(8,128)(2,1)}, bf16[1,8,1024]{2,1,0:T(8,128)(2,1)S(1)}, u32[]{:S(2)}, u32[]{:S(2)}) collective-permute-start(bf16[1,8,1024]{2,1,0:T(8,128)(2,1)} %bitcast.3), channel_id=1, source_target_pairs={{0,16},{2,18},{4,20},{6,22},{8,24},{10,26},{12,28},{14,30},{16,0},... | collective-permute-start | bytes 49160 | tf_op jit(solution)/shard_map/ppermute | solution.py:269
  4.7 1.9 %collective-permute-done.refs_1_ = bf16[1,8,1024]{2,1,0:T(8,128)(2,1)S(1)} collective-permute-done((bf16[1,8,1024]{2,1,0:T(8,128)(2,1)}, bf16[1,8,1024]{2,1,0:T(8,128)(2,1)S(1)}, u32[]{:S(2)}, u32[]{:S(2)}) %collective-permute-start) | collective-permute-done | bytes 16416 | tf_op jit(solution)/shard_map/ppermute | solution.py:269
  6.7 0.7 %pad_maximum_fusion.2 = bf16[2,8,1024]{2,1,0:T(8,128)(2,1)S(1)} fusion(bf16[1,8,1024]{2,1,0:T(8,128)(2,1)S(1)} %collective-permute-done.refs_1_, bf16[1,8,1024]{2,1,0:T(8,128)(2,1)} %bitcast.4), kind=kLoop, calls=%fused_computation.2 | loop fusion | flops 16384 | bytes 65536 | tf_op jit(solution)/shard_map/concatenate | solution.py:268
  7.4 1.9 %collective-permute-start.1 = (bf16[2,8,1024]{2,1,0:T(8,128)(2,1)S(1)}, bf16[2,8,1024]{2,1,0:T(8,128)(2,1)S(1)}, u32[]{:S(2)}, u32[]{:S(2)}) collective-permute-start(bf16[2,8,1024]{2,1,0:T(8,128)(2,1)S(1)} %pad_maximum_fusion.2), channel_id=1, source_target_pairs={{0,8},{2,10},{4,12},{6,14},{8,0},{10,2},{12,4},{14,6},{16,24},{18,... | collective-permute-start | bytes 98312 | tf_op jit(solution)/shard_map/ppermute | solution.py:269
  9.3 2.0 %collective-permute-done.1.refs_2_ = bf16[2,8,1024]{2,1,0:T(8,128)(2,1)S(1)} collective-permute-done((bf16[2,8,1024]{2,1,0:T(8,128)(2,1)S(1)}, bf16[2,8,1024]{2,1,0:T(8,128)(2,1)S(1)}, u32[]{:S(2)}, u32[]{:S(2)}) %collective-permute-start.1) | collective-permute-done | bytes 32800 | tf_op jit(solution)/shard_map/ppermute | solution.py:269
  11.3 0.7 %pad_maximum_fusion.1 = bf16[4,8,1024]{2,1,0:T(8,128)(2,1)S(1)} fusion(bf16[2,8,1024]{2,1,0:T(8,128)(2,1)S(1)} %collective-permute-done.1.refs_2_, bf16[1,8,1024]{2,1,0:T(8,128)(2,1)S(1)} %collective-permute-done.refs_1_, bf16[1,8,1024]{2,1,0:T(8,128)(2,1)} %bitcast.5), kind=kLoop, calls=%fused_computation.1 | loop fusion | flops 65536 | bytes 131072 | tf_op jit(solution)/shard_map/concatenate | solution.py:268
  12.0 1.9 %collective-permute-start.2 = (bf16[4,8,1024]{2,1,0:T(8,128)(2,1)S(1)}, bf16[4,8,1024]{2,1,0:T(8,128)(2,1)S(1)}, u32[]{:S(2)}, u32[]{:S(2)}) collective-permute-start(bf16[4,8,1024]{2,1,0:T(8,128)(2,1)S(1)} %pad_maximum_fusion.1), channel_id=1, source_target_pairs={{0,4},{2,6},{4,0},{6,2},{8,12},{10,14},{12,8},{14,10},{16,20},{18,... | collective-permute-start | bytes 196616 | tf_op jit(solution)/shard_map/ppermute | solution.py:269
  13.9 2.4 %collective-permute-done.2.refs_3_ = bf16[4,8,1024]{2,1,0:T(8,128)(2,1)S(1)} collective-permute-done((bf16[4,8,1024]{2,1,0:T(8,128)(2,1)S(1)}, bf16[4,8,1024]{2,1,0:T(8,128)(2,1)S(1)}, u32[]{:S(2)}, u32[]{:S(2)}) %collective-permute-start.2) | collective-permute-done | bytes 65568 | tf_op jit(solution)/shard_map/ppermute | solution.py:269
  16.3 0.7 %pad_maximum_fusion = bf16[8,8,1024]{2,1,0:T(8,128)(2,1)S(1)} fusion(bf16[4,8,1024]{2,1,0:T(8,128)(2,1)S(1)} %collective-permute-done.2.refs_3_, bf16[2,8,1024]{2,1,0:T(8,128)(2,1)S(1)} %collective-permute-done.1.refs_2_, bf16[1,8,1024]{2,1,0:T(8,128)(2,1)S(1)} %collective-permute-done.refs_1_, bf16[1,8,1024]{2,1,0:T(8,128)(2,1)} %bitcast.6), kind=kLoop, calls=%fused_computation | loop fusion | flops 196608 | bytes 262144 | tf_op jit(solution)/shard_map/concatenate | solution.py:268
  17.0 0.1 collective-permute-start.3
  17.1 2.0 %collective-permute-start.4 = (bf16[8,1024]{1,0:T(8,128)(2,1)}, bf16[8,1024]{1,0:T(8,128)(2,1)S(1)}, u32[]{:S(2)}, u32[]{:S(2)}) collective-permute-start(bf16[8,1024]{1,0:T(8,128)(2,1)} %vec.1), channel_id=1, source_target_pairs={{0,1},{1,0},{2,3},{3,2},{4,5},{5,4},{6,7},{7,6},{8,9},{9,8},{10,11... | collective-permute-start | bytes 49160 | tf_op jit(solution)/shard_map/ppermute | solution.py:257
  19.7 1.4 %collective-permute-done.4.refs_6_ = bf16[8,1024]{1,0:T(8,128)(2,1)S(1)} collective-permute-done((bf16[8,1024]{1,0:T(8,128)(2,1)}, bf16[8,1024]{1,0:T(8,128)(2,1)S(1)}, u32[]{:S(2)}, u32[]{:S(2)}) %collective-permute-start.4) | collective-permute-done | bytes 16416 | tf_op jit(solution)/shard_map/ppermute | solution.py:257
  21.1 0.0 collective-permute-done.3.refs_4_
  21.1 0.0 copy-start
  21.1 0.7 %copy-done = bf16[8,1024]{1,0:T(8,128)(2,1)S(1)} copy-done((bf16[8,1024]{1,0:T(8,128)(2,1)S(1)}, bf16[8,1024]{1,0:T(8,128)(2,1)}, u32[]{:S(2)}) %copy-start) | copy-done | bytes 16408
  21.9 3.9 %tile_work.1 = (f32[8,1024]{1,0:T(8,128)S(1)}, bf16[1,8,1024]{2,1,0:T(8,128)(2,1)S(1)}, f32[32,1,128]{2,1,0:T(1,128)}) custom-call(s32[1]{0:T(128)S(6)} %copy.8.count_s, s32[1024]{0:T(1024)} %rows_h.1, s32[1024]{0:T(1024)} %cols_h.1, f32[1,1024]{1,0:T(1,128)} %bitcast.9, bf16[1024,4096]{1,0:T(8,128)(2,1)} %tiles.1, bf16[1,8,1024]{2,1,0:T(8,128)(2,1)S(1)} %bitcast.7, ...), custom_call_target="tpu_custom_call" | custom-call | flops 67108864 | bytes 8388608 | tf_op jit(solution)/shard_map/tile_work/pallas_call | solution.py:187
  25.8 9.4 %all-to-all-start = ((f32[32,1,128]{2,1,0:T(1,128)}), f32[32,1,128]{2,1,0:T(1,128)S(1)}, u32[]{:S(2)}, u32[]{:S(2)}) async-start(f32[32,1,128]{2,1,0:T(1,128)} %get-tuple-element.6), calls=%async_computation | async-start | bytes 32768 | tf_op jit(solution)/shard_map/all_to_all | solution.py:306
  35.2 1.8 %collective-permute-start.5 = (bf16[8,1024]{1,0:T(8,128)(2,1)S(1)}, bf16[8,1024]{1,0:T(8,128)(2,1)S(1)}, u32[]{:S(2)}, u32[]{:S(2)}) collective-permute-start(bf16[8,1024]{1,0:T(8,128)(2,1)S(1)} %bitcast.8), channel_id=1, source_target_pairs={{0,1},{1,0},{2,3},{3,2},{4,5},{5,4},{6,7},{7,6},{8,9},{9,8},{10,11... | collective-permute-start | bytes 49160 | tf_op jit(solution)/shard_map/ppermute | solution.py:303
  37.0 2.0 %collective-permute-done.5.refs_0_ = bf16[8,1024]{1,0:T(8,128)(2,1)S(1)} collective-permute-done((bf16[8,1024]{1,0:T(8,128)(2,1)S(1)}, bf16[8,1024]{1,0:T(8,128)(2,1)S(1)}, u32[]{:S(2)}, u32[]{:S(2)}) %collective-permute-start.5) | collective-permute-done | bytes 16416 | tf_op jit(solution)/shard_map/ppermute | solution.py:303
  39.0 3.3 %all-to-all-done.gram_parts = f32[32,1,128]{2,1,0:T(1,128)S(1)} async-done(((f32[32,1,128]{2,1,0:T(1,128)}), f32[32,1,128]{2,1,0:T(1,128)S(1)}, u32[]{:S(2)}, u32[]{:S(2)}) %all-to-all-start) | async-done | bytes 16416 | tf_op jit(solution)/shard_map/all_to_all | solution.py:306
  42.3 0.0 copy-done.1
  42.3 0.8 %finish.1 = (bf16[8,1024]{1,0:T(8,128)(2,1)}, f32[8,1024]{1,0:T(8,128)}) custom-call(f32[8,1024]{1,0:T(8,128)S(1)} %get-tuple-element.5.base, f32[32,1,128]{2,1,0:T(1,128)S(1)} %all-to-all-done.gram_parts, bf16[8,1024]{1,0:T(8,128)(2,1)S(1)} %copy-done.1, bf16[8,1024]{1,0:T(8,128)(2,1)S(1)} %collective-permute-done.5.refs_0_), custom_call_target="tpu_custom_call" | custom-call | tf_op jit(solution)/shard_map/finish/pallas_call | solution.py:240
Async XLA Ops:
  0.6 41.7 %copy-start.1 = (bf16[8,1024]{1,0:T(8,128)(2,1)S(1)}, bf16[8,1024]{1,0:T(8,128)(2,1)}, u32[]{:S(2)}) copy-start(bf16[8,1024]{1,0:T(8,128)(2,1)} %vec.1) | copy-start | bytes 49156
  0.6 6.0 %collective-permute-start = (bf16[1,8,1024]{2,1,0:T(8,128)(2,1)}, bf16[1,8,1024]{2,1,0:T(8,128)(2,1)S(1)}, u32[]{:S(2)}, u32[]{:S(2)}) collective-permute-start(bf16[1,8,1024]{2,1,0:T(8,128)(2,1)} %bitcast.3), channel_id=1, source_target_pairs={{0,16},{2,18},{4,20},{6,22},{8,24},{10,26},{12,28},{14,30},{16,0},... | collective-permute-start | bytes 49160 | tf_op jit(solution)/shard_map/ppermute | solution.py:269
  7.4 3.9 %collective-permute-start.1 = (bf16[2,8,1024]{2,1,0:T(8,128)(2,1)S(1)}, bf16[2,8,1024]{2,1,0:T(8,128)(2,1)S(1)}, u32[]{:S(2)}, u32[]{:S(2)}) collective-permute-start(bf16[2,8,1024]{2,1,0:T(8,128)(2,1)S(1)} %pad_maximum_fusion.2), channel_id=1, source_target_pairs={{0,8},{2,10},{4,12},{6,14},{8,0},{10,2},{12,4},{14,6},{16,24},{18,... | collective-permute-start | bytes 98312 | tf_op jit(solution)/shard_map/ppermute | solution.py:269
  12.0 4.3 %collective-permute-start.2 = (bf16[4,8,1024]{2,1,0:T(8,128)(2,1)S(1)}, bf16[4,8,1024]{2,1,0:T(8,128)(2,1)S(1)}, u32[]{:S(2)}, u32[]{:S(2)}) collective-permute-start(bf16[4,8,1024]{2,1,0:T(8,128)(2,1)S(1)} %pad_maximum_fusion.1), channel_id=1, source_target_pairs={{0,4},{2,6},{4,0},{6,2},{8,12},{10,14},{12,8},{14,10},{16,20},{18,... | collective-permute-start | bytes 196616 | tf_op jit(solution)/shard_map/ppermute | solution.py:269
  17.0 4.1 %collective-permute-start.3 = (bf16[8,8,1024]{2,1,0:T(8,128)(2,1)S(1)}, bf16[8,8,1024]{2,1,0:T(8,128)(2,1)S(1)}, u32[]{:S(2)}, u32[]{:S(2)}) collective-permute-start(bf16[8,8,1024]{2,1,0:T(8,128)(2,1)S(1)} %pad_maximum_fusion), channel_id=1, source_target_pairs={{0,2},{2,0},{4,6},{6,4},{8,10},{10,8},{12,14},{14,12},{16,18},{18,... | collective-permute-start | bytes 393224 | tf_op jit(solution)/shard_map/ppermute | solution.py:269
  17.1 4.0 %collective-permute-start.4 = (bf16[8,1024]{1,0:T(8,128)(2,1)}, bf16[8,1024]{1,0:T(8,128)(2,1)S(1)}, u32[]{:S(2)}, u32[]{:S(2)}) collective-permute-start(bf16[8,1024]{1,0:T(8,128)(2,1)} %vec.1), channel_id=1, source_target_pairs={{0,1},{1,0},{2,3},{3,2},{4,5},{5,4},{6,7},{7,6},{8,9},{9,8},{10,11... | collective-permute-start | bytes 49160 | tf_op jit(solution)/shard_map/ppermute | solution.py:257
  21.1 0.7 %copy-start = (bf16[8,1024]{1,0:T(8,128)(2,1)S(1)}, bf16[8,1024]{1,0:T(8,128)(2,1)}, u32[]{:S(2)}) copy-start(bf16[8,1024]{1,0:T(8,128)(2,1)} %vec.1) | copy-start | bytes 49156
  25.8 16.5 %all-to-all-start = ((f32[32,1,128]{2,1,0:T(1,128)}), f32[32,1,128]{2,1,0:T(1,128)S(1)}, u32[]{:S(2)}, u32[]{:S(2)}) async-start(f32[32,1,128]{2,1,0:T(1,128)} %get-tuple-element.6), calls=%async_computation | async-start | bytes 32768 | tf_op jit(solution)/shard_map/all_to_all | solution.py:306
  35.2 3.8 %collective-permute-start.5 = (bf16[8,1024]{1,0:T(8,128)(2,1)S(1)}, bf16[8,1024]{1,0:T(8,128)(2,1)S(1)}, u32[]{:S(2)}, u32[]{:S(2)}) collective-permute-start(bf16[8,1024]{1,0:T(8,128)(2,1)S(1)} %bitcast.8), channel_id=1, source_target_pairs={{0,1},{1,0},{2,3},{3,2},{4,5},{5,4},{6,7},{7,6},{8,9},{9,8},{10,11... | collective-permute-start | bytes 49160 | tf_op jit(solution)/shard_map/ppermute | solution.py:303
